TPU v7x, 32 devices: a whole 2x2x4 slice. The times are simulated.
32 devices in a mesh: groups: 2 (over x), dp: 16 (over z, y, core).
Axes of the slice: x: 2, y: 2, z: 4, core: 2. Of those that a mesh axis runs over, the one named last changes fastest.
Arguments:
- x_input: bfloat16 [4096, 8192], P(('groups', 'dp')), parts along dimension 0, may hold values from -6 to 6
- bc_input: bfloat16 [4096, 1024], P(('groups', 'dp')), parts along dimension 0, may hold values from -3 to 3
- dt_input: bfloat16 [4096, 128], P(('groups', 'dp')), parts along dimension 0, may hold values from -3 to 3
- out_cotangent: bfloat16 [4096, 8192], P(('groups', 'dp')), parts along dimension 0, may hold values from -6 to 6
- prompt_states: bfloat16 [32, 8, 64, 128], P(('groups', 'dp')), parts along dimension 0, may hold values from -2 to 2
- prompt_tails: bfloat16 [32, 3, 576], P(('groups', 'dp')), parts along dimension 0, may hold values from -6 to 6
- rewards: float32 [32], P(('groups', 'dp')), parts along dimension 0, may hold values from 0 to 4
- lengths: int32 [32], P(('groups', 'dp')), parts along dimension 0, may hold values from 32 to 128, as said below
- owners: int32 [2, 16], P('groups'), parts along dimension 0, may hold values from 0 to 15, as said below
- conv_weight: float32 [4, 9216], replicated, may hold values from -3 to 3
- decay_log: float32 [128], replicated, may hold values from -7 to -2
- dt_bias: float32 [128], replicated, may hold values from -2 to 0
- skip_gain: float32 [128], replicated, may hold values from 0.5 to 1.5
Outputs:
- layer_output: bfloat16 [4096, 8192], P(('groups', 'dp')), parts along dimension 0
- state_grad: float32 [32, 8, 64, 128], P(('groups', 'dp')), parts along dimension 0
- tail_grad: float32 [32, 3, 576], P(('groups', 'dp')), parts along dimension 0
There are 2 independent parts, one for each index of `groups`. A program takes and returns all parts, laid end to end along the dimension named above; an argument that names none is the same for every part. Nothing has to cross between parts.
Inputs may be any that keep to these rules, and one draw needn't show every extreme that they name: owners lists each of 0 to 15 once. `lengths`: some response has all 128 tokens.
All inputs are finite; a program needn't handle non-finite values.
Results may differ from a plain program's by a relative error of at most 0.0031.
Values may be sent and summed in bfloat16 or wider, within the bound.
A program may use at most 128 MiB of HBM per device.

v0:
```python
import jax
import jax.numpy as jnp
from jax import lax
from jax.experimental import pallas as pl
from jax.experimental.pallas import tpu as pltpu
from jax.sharding import PartitionSpec as P

highest = lax.Precision.HIGHEST
f32 = jnp.float32
bf16 = jnp.bfloat16


def split(a):
    hi = a.astype(bf16)
    return hi, (a - hi.astype(f32)).astype(bf16)


def dot(a, b, dims):
    return lax.dot_general(a, b, (dims, ((), ())), preferred_element_type=f32)


def widen(cols, head_size):
    rows, heads = cols.shape
    return jnp.concatenate(
        [jnp.broadcast_to(cols[:, h : h + 1], (rows, head_size)) for h in range(heads)], axis=1
    )


def within_kernel(
    blocks_per_group, head_size, lags, own, x_ref, cot_ref, tail_ref, conv_ref, cumc_ref, cumr_ref,
    delr_ref, wt_ref, skip_ref, score_ref, cc_ref, y_ref, dst_ref, dtail_ref, dscore_ref, ext,
):
    j = pl.program_id(0)
    rows = x_ref.shape[0]
    heads = cumc_ref.shape[2]
    state_size = score_ref.shape[2]
    ext[0:8, :] = tail_ref[...]
    ext[8:, :] = x_ref[...].astype(f32)
    conv = conv_ref[...]
    u = conv[0:1] * ext[8 - lags : 8 - lags + rows, :]
    for k in range(1, lags + 1):
        u = u + conv[k : k + 1] * ext[8 - lags + k : 8 - lags + k + rows, :]
    sig = 1.0 / (1.0 + jnp.exp(-u))
    act = u * sig
    act_hi, act_lo = split(act)
    cumc = cumc_ref[0]
    weight = wt_ref[...]
    score = score_ref[0]
    cot = cot_ref[...]
    parts, dvals = [], []
    dscore = jnp.zeros((rows, 8), f32)
    for h in range(heads):
        lanes = slice(h * head_size, (h + 1) * head_size)
        gap = cumc[:, h : h + 1] - cumr_ref[0, h : h + 1, :]
        decay = jnp.exp(jnp.minimum(gap, 0.0)) * delr_ref[0, h : h + 1, :]
        mix = decay * score
        mix_hi, mix_lo = split(mix)
        hi, lo = act_hi[:, lanes], act_lo[:, lanes]
        wide = dot(mix_hi, jnp.concatenate([hi, lo], axis=1), ((1,), (0,)))
        part = wide[:, :head_size] + wide[:, head_size:] + dot(mix_lo, hi, ((1,), (0,)))
        parts.append(part)
        mw_hi, mw_lo = split(mix[:, :8] * weight)
        cot_h = cot[:, lanes]
        both = dot(jnp.concatenate([mw_hi, mw_lo], axis=1), cot_h, ((0,), (0,)))
        dvals.append(both[:8] + both[8:])
        q = dot(cot_h, hi[:8], ((1,), (1,))) + dot(cot_h, lo[:8], ((1,), (1,)))
        dscore = dscore + decay[:, :8] * q
    skip = skip_ref[...]
    y_ref[...] = jnp.concatenate(parts, axis=1) + skip * act
    dscore = dscore * weight

    @pl.when(lax.rem(j, blocks_per_group) == 0)
    def _():
        dscore_ref[0] = dscore

    @pl.when(lax.rem(j, blocks_per_group) != 0)
    def _():
        dscore_ref[0] += dscore

    cot32 = cot.astype(f32)
    z_hi, z_lo = split(cot32 * widen(jnp.exp(cumc) * weight, head_size))
    cc = cc_ref[0]
    wide = dot(z_hi, cc, ((0,), (0,)))
    dst = wide[:, :state_size] + wide[:, state_size:] + dot(z_lo, cc[:, :state_size], ((0,), (0,)))
    dst_ref[0] = dst.astype(bf16)

    dact = jnp.concatenate(dvals, axis=1) + skip * cot32[:8] * weight[:8]
    u8, s8 = u[:8], sig[:8]
    dtail_ref[...] = dact * (s8 * (1.0 + u8 * (1.0 - s8)))


def carried_kernel(
    blocks_per_group, head_size, own, y_ref, cot_ref, cumc_ref, wt_ref, cc_ref, state_ref, out_ref, dc_ref
):
    j = pl.program_id(0)
    state_size = state_ref.shape[2]
    state = state_ref[0]
    cc = cc_ref[0]
    carried = dot(cc[:, :state_size], state, ((1,), (1,))) + dot(
        cc[:, state_size:], state, ((1,), (1,))
    )
    gains = jnp.exp(cumc_ref[0])
    wide = widen(gains, head_size)
    out_ref[...] = (y_ref[...] + wide * carried).astype(bf16)
    z = cot_ref[...][:8].astype(f32) * (wide[:8] * wt_ref[...][:8])
    z_hi, z_lo = split(z)
    dc = dot(z_hi, state, ((1,), (0,))) + dot(z_lo, state, ((1,), (0,)))

    @pl.when(lax.rem(j, blocks_per_group) == 0)
    def _():
        dc_ref[0] = dc

    @pl.when(lax.rem(j, blocks_per_group) != 0)
    def _():
        dc_ref[0] += dc


def spread(a, count):
    return lax.all_to_all(
        jnp.broadcast_to(a[None], (count,) + a.shape), "dp", split_axis=0, concat_axis=0, tiled=True
    )


def local(
    x_input, bc_input, dt_input, out_cotangent, prompt_states, prompt_tails, rewards, lengths,
    owners, conv_weight, decay_log, dt_bias, skip_gain,
):
    device_count = lax.axis_size("dp")
    my_index = lax.axis_index("dp")
    prompt_count, resp_count = owners.shape
    _, block_heads, head_size, state_size = prompt_states.shape
    lags, tail_width = prompt_tails.shape[1:]
    rows, inner = x_input.shape
    heads = dt_input.shape[1]
    group_width = bc_input.shape[1] // 2
    groups = group_width // state_size
    width = block_heads * head_size
    per_group = resp_count // groups
    tail_len = lags * tail_width
    holder_ids = jnp.arange(device_count, dtype=jnp.int32)
    prompt_ids = jnp.arange(prompt_count, dtype=jnp.int32)

    small = jnp.concatenate([prompt_tails.reshape(-1).astype(f32), rewards.astype(f32)])
    small = spread(jnp.pad(small, (0, -small.shape[0] % 128)), device_count)
    states = spread(prompt_states.reshape(width, state_size), device_count)

    matches = owners[:, :, None] == holder_ids[None, None, :]
    held_prompt = jnp.sum(jnp.where(matches, prompt_ids[:, None, None], 0), axis=(0, 1))
    my_prompt = jnp.sum(jnp.where(holder_ids == my_index, held_prompt, 0))
    owner_row = jnp.sum(jnp.where((prompt_ids == my_prompt)[:, None], owners, 0), axis=0)
    pick = (owner_row[:, None] == holder_ids[None, :]).astype(f32)

    member = (held_prompt == my_prompt).astype(f32)
    reward_all = small[:, tail_len]
    mean_value = jnp.sum(member * reward_all) / resp_count
    spread_value = jnp.sum(member * (reward_all - mean_value) ** 2) / resp_count
    advantage = (rewards[0] - mean_value) / jnp.maximum(jnp.sqrt(spread_value), 1.0)
    length = lengths[0]
    alive = (jnp.arange(rows, dtype=jnp.int32) < length).astype(f32)
    weight = (advantage * alive / length.astype(f32))[:, None]

    tails = jnp.dot(pick, small[:, :tail_len], precision=highest)
    tails = tails.reshape(resp_count, lags, tail_width).transpose(1, 0, 2).reshape(lags, -1)

    bc_ext = jnp.concatenate([tails[:, inner:], bc_input.astype(f32)], axis=0)
    bc_conv = conv_weight[:, inner:]
    bc_u = bc_conv[0][None] * bc_ext[0:rows]
    for k in range(1, lags + 1):
        bc_u = bc_u + bc_conv[k][None] * bc_ext[k : k + rows]
    bc_act = jax.nn.silu(bc_u)
    b_proj = bc_act[:, :group_width].reshape(rows, groups, state_size)
    c_proj = bc_act[:, group_width:].reshape(rows, groups, state_size)
    causal = jnp.arange(rows)[:, None] >= jnp.arange(rows)[None, :]
    scores = jnp.einsum("tgn,sgn->gts", c_proj, b_proj, precision=highest)
    scores = jnp.where(causal[None], scores, 0.0)
    c_group = c_proj.transpose(1, 0, 2)
    c_hi, c_lo = split(c_group)
    cc = jnp.concatenate([c_hi, c_lo], axis=2)

    step_size = jax.nn.softplus(dt_input.astype(f32) + dt_bias[None, :])
    decrement = -step_size * jnp.exp(decay_log)[None, :]
    cumulative = jnp.dot(causal.astype(f32), decrement, precision=highest)
    cumc = cumulative.reshape(rows, resp_count, block_heads).transpose(1, 0, 2)
    cumr = cumulative.T.reshape(resp_count, block_heads, rows)
    delr = step_size.T.reshape(resp_count, block_heads, rows)
    skip = jnp.repeat(skip_gain, head_size)[None, :]
    tail8 = jnp.pad(tails[:, :inner], ((8 - lags, 0), (0, 0)))
    conv_x = conv_weight[:, :inner]
    taps = conv_x.shape[0]

    wide_spec = pl.BlockSpec((rows, width), lambda j, own: (0, j))
    cumc_spec = pl.BlockSpec((1, rows, block_heads), lambda j, own: (j, 0, 0))
    row_spec = pl.BlockSpec((1, block_heads, rows), lambda j, own: (j, 0, 0))
    wt_spec = pl.BlockSpec((rows, 1), lambda j, own: (0, 0))
    cc_spec = pl.BlockSpec((1, rows, 2 * state_size), lambda j, own: (j // per_group, 0, 0))
    slot_spec = pl.BlockSpec((1, width, state_size), lambda j, own: (own[j], 0, 0))
    eight = pl.BlockSpec((8, width), lambda j, own: (0, j))

    y_part, dstate, du_x, dscore = pl.pallas_call(
        lambda *refs: within_kernel(per_group, head_size, lags, *refs),
        grid_spec=pltpu.PrefetchScalarGridSpec(
            num_scalar_prefetch=1,
            grid=(resp_count,),
            in_specs=[
                wide_spec,
                wide_spec,
                eight,
                pl.BlockSpec((taps, width), lambda j, own: (0, j)),
                cumc_spec,
                row_spec,
                row_spec,
                wt_spec,
                pl.BlockSpec((1, width), lambda j, own: (0, j)),
                pl.BlockSpec((1, rows, rows), lambda j, own: (j // per_group, 0, 0)),
                cc_spec,
            ],
            out_specs=[
                wide_spec,
                slot_spec,
                eight,
                pl.BlockSpec((1, rows, 8), lambda j, own: (j // per_group, 0, 0)),
            ],
            scratch_shapes=[pltpu.VMEM((rows + 8, width), f32)],
        ),
        out_shape=[
            jax.ShapeDtypeStruct((rows, inner), f32),
            jax.ShapeDtypeStruct((device_count, width, state_size), bf16),
            jax.ShapeDtypeStruct((8, inner), f32),
            jax.ShapeDtypeStruct((groups, rows, 8), f32),
        ],
        compiler_params=pltpu.CompilerParams(vmem_limit_bytes=24 << 20),
        cost_estimate=pl.CostEstimate(flops=3 << 30, bytes_accessed=12 << 20, transcendentals=4 << 20),
        name="within",
    )(owner_row, x_input, out_cotangent, tail8, conv_x, cumc, cumr, delr, weight, skip, scores, cc)

    if prompt_count > 1:
        dstate = jnp.where((held_prompt == my_prompt)[:, None, None], dstate, jnp.zeros_like(dstate))
    got = lax.all_to_all(dstate, "dp", split_axis=0, concat_axis=0, tiled=True)

    layer_out, dc_state = pl.pallas_call(
        lambda *refs: carried_kernel(per_group, head_size, *refs),
        grid_spec=pltpu.PrefetchScalarGridSpec(
            num_scalar_prefetch=1,
            grid=(resp_count,),
            in_specs=[wide_spec, pl.BlockSpec((16, width), lambda j, own: (0, j)), cumc_spec, wt_spec, cc_spec, slot_spec],
            out_specs=[
                wide_spec,
                pl.BlockSpec((1, 8, state_size), lambda j, own: (j // per_group, 0, 0)),
            ],
        ),
        out_shape=[
            jax.ShapeDtypeStruct((rows, inner), bf16),
            jax.ShapeDtypeStruct((groups, 8, state_size), f32),
        ],
        compiler_params=pltpu.CompilerParams(vmem_limit_bytes=24 << 20),
        cost_estimate=pl.CostEstimate(flops=1 << 30, bytes_accessed=9 << 20, transcendentals=1 << 17),
        name="carried",
    )(owner_row, y_part, out_cotangent, cumc, weight, cc, states)

    keep = jnp.where(causal[:, :8][None], dscore, 0.0)
    db = jnp.einsum("gts,gtn->sgn", keep, c_group, precision=highest).reshape(8, group_width)
    dc = jnp.einsum("gts,sgn->tgn", keep[:, :8], b_proj[:8], precision=highest)
    dc = (dc + dc_state.transpose(1, 0, 2)).reshape(8, group_width)
    sig = jax.nn.sigmoid(bc_u[:8])
    du_bc = jnp.concatenate([db, dc], axis=1) * (sig * (1.0 + bc_u[:8] * (1.0 - sig)))
    du = jnp.concatenate([du_x, du_bc], axis=1)
    dtail = jnp.stack(
        [sum(conv_weight[m - t] * du[t] for t in range(m + 1)) for m in range(lags)]
    ).astype(bf16)
    tail_blocks = dtail.reshape(lags, resp_count, tail_width).transpose(1, 0, 2)
    tail_blocks = tail_blocks.reshape(resp_count, tail_len)
    tail_send = jnp.dot(pick.T.astype(bf16), tail_blocks, preferred_element_type=f32).astype(bf16)
    got_tail = lax.all_to_all(tail_send, "dp", split_axis=0, concat_axis=0, tiled=True)

    state_grad = jnp.sum(got.astype(f32), axis=0)
    state_grad = state_grad.reshape(1, block_heads, head_size, state_size)
    tail_grad = jnp.sum(got_tail.astype(f32), axis=0).reshape(1, lags, tail_width)
    return layer_out, state_grad, tail_grad


def solution(mesh):
    in_specs = (
        P(("groups", "dp"), None),
        P(("groups", "dp"), None),
        P(("groups", "dp"), None),
        P(("groups", "dp"), None),
        P(("groups", "dp"), None, None, None),
        P(("groups", "dp"), None, None),
        P(("groups", "dp")),
        P(("groups", "dp")),
        P("groups", None),
        P(),
        P(),
        P(),
        P(),
    )
    out_specs = (
        P(("groups", "dp"), None),
        P(("groups", "dp"), None, None, None),
        P(("groups", "dp"), None, None),
    )
    return jax.shard_map(local, mesh=mesh, in_specs=in_specs, out_specs=out_specs, check_vma=False)
```

profile of v0, /device:TPU:13, one launch (start us, length us, event | category | flops | bytes accessed | tf_op | source)
XLA Modules:
  0.0 169.8 jit_solution(772586311221280015)
XLA Ops:
  2.2 11.3 %all_to_all.28 = f32[16,1,1792]{2,1,0:T(1,128)S(1)} all-to-all(f32[16,1,1792]{2,1,0:T(1,128)S(1)} %broadcast_in_dim.46), channel_id=1, replica_groups=mesh['groups'=2,'dp'=16] {'dp'}, dimensions={0} | all-to-all | bytes 229376 | tf_op jit(solution)/shard_map/all_to_all | solution.py:119
  13.5 2.6 %broadcast_in_dim.75 = bf16[16,512,128]{2,1,0:T(8,128)(2,1)} broadcast(bf16[512,128]{1,0:T(8,128)(2,1)} %bitcast.78), dimensions={1,2} | broadcast | bytes 2228224 | tf_op jit(solution)/shard_map/broadcast_in_dim | solution.py:120
  16.1 6.5 %all-to-all-start.1 = ((bf16[16,512,128]{2,1,0:T(8,128)(2,1)}), bf16[16,512,128]{2,1,0:T(8,128)(2,1)S(1)}, u32[]{:S(2)}, u32[]{:S(2)}) async-start(bf16[16,512,128]{2,1,0:T(8,128)(2,1)} %broadcast_in_dim.75), calls=%async_computation.1 | async-start | bytes 4194304 | tf_op jit(solution)/shard_map/all_to_all | solution.py:119
  28.4 1.2 copy.69
  29.7 1.7 %fusion.3 = f32[16,1728]{1,0:T(8,128)S(1)} fusion(f32[16,1792]{0,1:T(8,128)} %bitcast.70, s32[16]{0:T(128)S(1)} %bitcast.66), kind=kOutput, calls=%fused_computation.8 | convolution fusion | flops 5308672 | bytes 995392 | tf_op jit(solution)/shard_map/dot_general | solution.py:162
  32.4 2.8 %divide_multiply_fusion = (f32[128,1024]{1,0:T(8,128)S(1)}, f32[128,1024]{1,0:T(8,128)}) fusion(f32[128,1024]{1,0:T(8,128)} %convert_element_type.54, f32[1024]{0:T(1024)S(1)} %bitcast.82, f32[3,1024]{1,0:T(4,128)S(1)} %slice.116, f32[1024]{0:T(1024)S(1)} %bitcast.80, f32[1024]{0:T(1024)S(1)} %bitcast.81, f32[1024]{0:T(1024)S(1)} %bitcast.79), kind=kLoop, calls=%fused_computation.23 | loop fusion | flops 1835008 | bytes 1601536 | tf_op jit(solution)/shard_map/jit(silu)/mul | solution.py:170
  36.2 1.1 copy.73
  38.1 1.3 slice_reduce_fusion
  40.0 1.3 multiply_reduce_fusion
  42.0 1.1 pad.9.refs_3_
  43.1 1.0 fusion.16
  44.1 1.6 convolution_select_fusion.refs_10_
  45.8 0.9 copy-done.7
  48.3 1.6 copy-done.11
  49.9 33.2 %within.1 = (f32[128,8192]{1,0:T(8,128)S(1)}, bf16[16,512,128]{2,1,0:T(8,128)(2,1)S(1)}, f32[8,8192]{1,0:T(8,128)S(1)}, f32[4,128,8]{2,1,0:T(8,128)S(1)}) custom-call(s32[16]{0:T(128)S(1)} %bitcast.67, bf16[128,8192]{1,0:T(8,128)(2,1)S(1)} %copy-done.11, bf16[128,8192]{1,0:T(8,128)(2,1)S(1)} %copy-done.2, f32[8,8192]{1,0:T(8,128)S(1)} %pad.9.refs_3_, ...), custom_call_target="tpu_custom_call" | custom-call | flops 3221225472 | bytes 12582912 | tf_op jit(solution)/shard_map/within/pallas_call | solution.py:199
  83.1 1.9 %copy-done = f32[128,8192]{1,0:T(8,128)} copy-done((f32[128,8192]{1,0:T(8,128)}, f32[128,8192]{1,0:T(8,128)S(1)}, u32[]{:S(2)}) %copy-start) | copy-done | bytes 4194328
  85.1 1.3 copy-done.4
  88.4 2.2 %copy-done.1 = f32[128,8192]{1,0:T(8,128)S(1)} copy-done((f32[128,8192]{1,0:T(8,128)S(1)}, f32[128,8192]{1,0:T(8,128)}, u32[]{:S(2)}) %copy-start.1) | copy-done | bytes 4194328
  90.6 1.6 copy-done.3
  92.1 8.7 %carried.1 = (bf16[128,8192]{1,0:T(8,128)(2,1)}, f32[4,8,128]{2,1,0:T(8,128)S(1)}) custom-call(s32[16]{0:T(128)S(1)} %bitcast.68, f32[128,8192]{1,0:T(8,128)S(1)} %copy-done.1, bf16[128,8192]{1,0:T(8,128)(2,1)S(1)} %copy-done.3, f32[16,128,8]{2,1,0:T(8,128)S(1)} %bitcast.62, f32[128,1]{1,0:T(8,128)S(1)} %select_divide_fusion.refs_8_.refs_4_, ...), custom_call_target="tpu_custom_call" | custom-call | flops 1073741824 | bytes 9437184 | tf_op jit(solution)/shard_map/carried/pallas_call | solution.py:240
  105.0 10.1 %all_to_all.29 = bf16[16,2,864]{2,1,0:T(2,128)(2,1)S(1)} all-to-all(bf16[16,2,864]{2,1,0:T(2,128)(2,1)S(1)} %reshape.135), channel_id=1, replica_groups=mesh['groups'=2,'dp'=16] {'dp'}, dimensions={0} | all-to-all | bytes 110592 | tf_op jit(solution)/shard_map/all_to_all | solution.py:273
  115.1 6.2 %all-to-all-start.2 = ((bf16[16,512,128]{2,1,0:T(8,128)(2,1)}), bf16[16,512,128]{2,1,0:T(8,128)(2,1)S(1)}, u32[]{:S(2)}, u32[]{:S(2)}) async-start(bf16[16,512,128]{2,1,0:T(8,128)(2,1)} %copy-done.4), calls=%async_computation.2 | async-start | bytes 4194304 | tf_op jit(solution)/shard_map/all_to_all | solution.py:238
  122.3 46.5 %all-to-all-done.2 = bf16[16,512,128]{2,1,0:T(8,128)(2,1)S(1)} async-done(((bf16[16,512,128]{2,1,0:T(8,128)(2,1)}), bf16[16,512,128]{2,1,0:T(8,128)(2,1)S(1)}, u32[]{:S(2)}, u32[]{:S(2)}) %all-to-all-start.2) | async-done | bytes 2097184 | tf_op jit(solution)/shard_map/all_to_all | solution.py:238
  168.8 1.0 convert_reduce_fusion
  (83 shorter events, 17.4 us)
Async XLA Ops:
  16.1 6.5 %copy-start.18 = (bf16[128,1024]{1,0:T(8,128)(2,1)S(1)}, bf16[128,1024]{1,0:T(8,128)(2,1)}, u32[]{:S(2)}) copy-start(bf16[128,1024]{1,0:T(8,128)(2,1)} %param.14) | copy-start | bytes 786436
  16.1 8.1 %copy-start.23 = (f32[128]{0:T(128)S(1)}, f32[128]{0:T(128)}, u32[]{:S(2)}) copy-start(f32[128]{0:T(128)} %param.23) | copy-start | bytes 1540
  16.1 8.1 %copy-start.20 = (bf16[128,128]{1,0:T(8,128)(2,1)S(1)}, bf16[128,128]{1,0:T(8,128)(2,1)}, u32[]{:S(2)}) copy-start(bf16[128,128]{1,0:T(8,128)(2,1)} %param.15) | copy-start | bytes 98308
  16.1 8.1 %copy-start.21 = (f32[128]{0:T(128)S(1)}, f32[128]{0:T(128)}, u32[]{:S(2)}) copy-start(f32[128]{0:T(128)} %param.24) | copy-start | bytes 1540
  16.1 72.3 %all-to-all-start.1 = ((bf16[16,512,128]{2,1,0:T(8,128)(2,1)}), bf16[16,512,128]{2,1,0:T(8,128)(2,1)S(1)}, u32[]{:S(2)}, u32[]{:S(2)}) async-start(bf16[16,512,128]{2,1,0:T(8,128)(2,1)} %broadcast_in_dim.75), calls=%async_computation.1 | async-start | bytes 4194304 | tf_op jit(solution)/shard_map/all_to_all | solution.py:119
  22.6 3.7 %copy-start.16 = (f32[4,9216]{1,0:T(4,128)S(1)}, f32[4,9216]{1,0:T(4,128)}, u32[]{:S(2)}) copy-start(f32[4,9216]{1,0:T(4,128)} %param.22) | copy-start | bytes 442372
  22.7 4.4 %copy-start.22 = (f32[128]{0:T(128)S(1)}, f32[128]{0:T(128)}, u32[]{:S(2)}) copy-start(f32[128]{0:T(128)} %param.25) | copy-start | bytes 1540
  22.7 7.0 %copy-start.10 = (s32[1,16]{1,0:T(1,128)S(1)}, s32[1,16]{1,0:T(1,128)}, u32[]{:S(2)}) copy-start(s32[1,16]{1,0:T(1,128)} %param.21) | copy-start | bytes 196
  35.3 1.0 copy-start.14
  37.3 5.8 %copy-start.12 = (f32[128,512]{0,1:T(8,128)}, f32[128,512]{0,1:T(8,128)S(1)}, u32[]{:S(2)}) copy-start(f32[128,512]{0,1:T(8,128)S(1)} %copy.73) | copy-start | bytes 786436
  41.9 3.8 %copy-start.2 = (bf16[128,8192]{1,0:T(8,128)(2,1)S(1)}, bf16[128,8192]{1,0:T(8,128)(2,1)}, u32[]{:S(2)}) copy-start(bf16[128,8192]{1,0:T(8,128)(2,1)} %refs_2_.3) | copy-start | bytes 6291460
  45.8 0.9 copy-start.7
  46.7 0.8 copy-start.8
  47.5 0.8 copy-start.9
  48.3 1.6 copy-start.11
  49.9 36.5 %copy-start.19 = (pred[128,128]{1,0:T(8,128)(4,1)S(1)}, pred[128,128]{1,0:T(8,128)(4,1)}, u32[]{:S(2)}) copy-start(pred[128,128]{1,0:T(8,128)(4,1)} %iota_compare_fusion.1) | copy-start | bytes 49156
  49.9 37.9 %copy-start.13 = (f32[128,4,128]{2,0,1:T(8,128)S(1)}, f32[128,4,128]{2,0,1:T(8,128)}, u32[]{:S(2)}) copy-start(f32[128,4,128]{2,0,1:T(8,128)} %copy.76) | copy-start | bytes 786436
  83.1 2.0 %copy-start = (f32[128,8192]{1,0:T(8,128)}, f32[128,8192]{1,0:T(8,128)S(1)}, u32[]{:S(2)}) copy-start(f32[128,8192]{1,0:T(8,128)S(1)} %get-tuple-element.9.refs_1_) | copy-start | bytes 12582916
  85.1 1.3 copy-start.4
  88.4 2.2 %copy-start.1 = (f32[128,8192]{1,0:T(8,128)S(1)}, f32[128,8192]{1,0:T(8,128)}, u32[]{:S(2)}) copy-start(f32[128,8192]{1,0:T(8,128)} %copy-done) | copy-start | bytes 12582916
  90.6 1.6 copy-start.3
  92.1 10.4 %copy-start.6 = (f32[8,8192]{1,0:T(8,128)S(1)}, f32[8,8192]{1,0:T(8,128)}, u32[]{:S(2)}) copy-start(f32[8,8192]{1,0:T(8,128)} %copy-done.5) | copy-start | bytes 786436
  92.1 10.4 %copy-start.17 = (f32[4,9216]{1,0:T(4,128)S(1)}, f32[4,9216]{1,0:T(4,128)}, u32[]{:S(2)}) copy-start(f32[4,9216]{1,0:T(4,128)} %param.22) | copy-start | bytes 442372
  115.1 53.7 %all-to-all-start.2 = ((bf16[16,512,128]{2,1,0:T(8,128)(2,1)}), bf16[16,512,128]{2,1,0:T(8,128)(2,1)S(1)}, u32[]{:S(2)}, u32[]{:S(2)}) async-start(bf16[16,512,128]{2,1,0:T(8,128)(2,1)} %copy-done.4), calls=%async_computation.2 | async-start | bytes 4194304 | tf_op jit(solution)/shard_map/all_to_all | solution.py:238
  (2 other events, 1.4 us)
where the time goes:
time: 171 us; the launch traced here: 170 us
  waiting for transfers between devices  46.5 us (27%)
  Pallas kernels  42 us (25%)
  local copies, waits for them, and re-layouts  26.5 us (15%)
  blocking collectives  21.4 us (13%)
  starting transfers between devices  12.8 us (7%)
  other arithmetic  11.9 us (7%)
  matrix products  5.21 us (3%)
  between operations  3.48 us (2%)
    all_to_all x1, waiting for transfers between devices, local(): got = lax.all_to_all(dstate, 'dp', split_axis=0, concat_axis=0, tiled=True)  46.5 us
    pallas_call x1, Pallas kernels, local(): pl.pallas_call(lambda *refs: within_kernel(per_group, head_size, lags, *r...  33.2 us
    unnamed x51, local copies, waits for them, and re-layouts  13.8 us
    all_to_all x1, blocking collectives, spread(): lax.all_to_all(jnp.broadcast_to(a[None], (count,) + a.shape), 'dp', split...  11.3 us
    all_to_all x1, blocking collectives, local(): lax.all_to_all(tail_send, 'dp', split_axis=0, concat_axis=0, tiled=True)  10.1 us
    pallas_call x1, Pallas kernels, local(): pl.pallas_call(lambda *refs: carried_kernel(per_group, head_size, *refs),...  8.72 us
    all_to_all x1, starting transfers between devices, spread(): lax.all_to_all(jnp.broadcast_to(a[None], (count,) + a.shape), 'dp', split...  6.53 us
    all_to_all x1, starting transfers between devices, local(): got = lax.all_to_all(dstate, 'dp', split_axis=0, concat_axis=0, tiled=True)  6.24 us
  transfers between devices with their start and end apart: 2, of which 1 were waited for; matrix products, arithmetic and copies ran while one was open for 13% of the time, Pallas kernels for 20%

commit v1 on v0

--- a/solution.py
+++ b/solution.py
@@ -26,14 +26,111 @@
     )
 
 
+def exchange_kernel(count, src_ref, out_ref, send_sem, recv_sem, own_sem):
+    me = lax.axis_index("dp")
+    barrier = pltpu.get_barrier_semaphore()
+
+    def greet(step, carry):
+        peer = lax.rem(me + step, count)
+        pl.semaphore_signal(
+            barrier, inc=1, device_id={"dp": peer}, device_id_type=pl.DeviceIdType.MESH
+        )
+        return carry
+
+    lax.fori_loop(1, count, greet, 0)
+    pl.semaphore_wait(barrier, count - 1)
+
+    def copy(step):
+        peer = lax.rem(me + step, count)
+        return pltpu.make_async_remote_copy(
+            src_ref=src_ref.at[peer],
+            dst_ref=out_ref.at[me],
+            send_sem=send_sem.at[step],
+            recv_sem=recv_sem.at[step],
+            device_id={"dp": peer},
+            device_id_type=pl.DeviceIdType.MESH,
+        )
+
+    def start(step, carry):
+        copy(step).start()
+        return carry
+
+    def finish(step, carry):
+        copy(step).wait()
+        return carry
+
+    lax.fori_loop(1, count, start, 0)
+    mine = pltpu.make_async_copy(src_ref.at[me], out_ref.at[me], own_sem)
+    mine.start()
+    mine.wait()
+    lax.fori_loop(1, count, finish, 0)
+
+
+def exchange(a, count, collective_id):
+    return pl.pallas_call(
+        lambda *refs: exchange_kernel(count, *refs),
+        out_shape=jax.ShapeDtypeStruct(a.shape, a.dtype),
+        in_specs=[pl.BlockSpec(memory_space=pltpu.VMEM)],
+        out_specs=pl.BlockSpec(memory_space=pltpu.VMEM),
+        scratch_shapes=[
+            pltpu.SemaphoreType.DMA((count,)),
+            pltpu.SemaphoreType.DMA((count,)),
+            pltpu.SemaphoreType.DMA,
+        ],
+        compiler_params=pltpu.CompilerParams(
+            collective_id=collective_id, has_side_effects=True, vmem_limit_bytes=16 << 20
+        ),
+        cost_estimate=pl.CostEstimate(flops=0, bytes_accessed=12 << 20, transcendentals=0),
+        name="exchange",
+    )(a)
+
+
+def prepare_kernel(
+    groups, state_size, lags, dt_ref, bias_ref, decay_ref, bc_ref, tail_ref, conv_ref,
+    cum_ref, step_ref, score_ref, scoret_ref, cc_ref, act_ref, u8_ref, ext,
+):
+    rows = dt_ref.shape[0]
+    row = lax.broadcasted_iota(jnp.int32, (rows, rows), 0)
+    col = lax.broadcasted_iota(jnp.int32, (rows, rows), 1)
+    logits = dt_ref[...].astype(f32) + bias_ref[...]
+    step = jnp.maximum(logits, 0.0) + jnp.log1p(jnp.exp(-jnp.abs(logits)))
+    dec = -step * jnp.exp(decay_ref[...])
+    step_ref[...] = step.T
+    cum_ref[...] = lax.dot_general(
+        dec.T, jnp.where(row <= col, 1.0, 0.0), (((1,), (0,)), ((), ())),
+        precision=highest, preferred_element_type=f32,
+    )
+    ext[0:8, :] = tail_ref[...]
+    ext[8:, :] = bc_ref[...].astype(f32)
+    conv = conv_ref[...]
+    u = conv[0:1] * ext[8 - lags : 8 - lags + rows, :]
+    for k in range(1, lags + 1):
+        u = u + conv[k : k + 1] * ext[8 - lags + k : 8 - lags + k + rows, :]
+    u8_ref[...] = u[:8]
+    act = u * (1.0 / (1.0 + jnp.exp(-u)))
+    act_ref[...] = act
+    for g in range(groups):
+        b = act[:, g * state_size : (g + 1) * state_size]
+        c = act[:, (groups + g) * state_size : (groups + g + 1) * state_size]
+        score = lax.dot_general(
+            c, b, (((1,), (1,)), ((), ())), precision=highest, preferred_element_type=f32
+        )
+        score = jnp.where(row >= col, score, 0.0)
+        score_ref[g] = score
+        scoret_ref[g] = score.T[:8]
+        hi, lo = split(c)
+        cc_ref[g, :, :state_size] = hi
+        cc_ref[g, :, state_size:] = lo
+
+
 def within_kernel(
-    blocks_per_group, head_size, lags, own, x_ref, cot_ref, tail_ref, conv_ref, cumc_ref, cumr_ref,
-    delr_ref, wt_ref, skip_ref, score_ref, cc_ref, y_ref, dst_ref, dtail_ref, dscore_ref, ext,
+    blocks_per_group, head_size, lags, own, x_ref, cot_ref, tail_ref, conv_ref, cumr_ref,
+    delr_ref, wt_ref, wrow_ref, skip_ref, score_ref, scoret_ref, cc_ref, y_ref, dst_ref, dtail_ref, dscore_ref, ext,
 ):
     j = pl.program_id(0)
     rows = x_ref.shape[0]
-    heads = cumc_ref.shape[2]
-    state_size = score_ref.shape[2]
+    heads = cumr_ref.shape[0]
+    state_size = cc_ref.shape[2] // 2
     ext[0:8, :] = tail_ref[...]
     ext[8:, :] = x_ref[...].astype(f32)
     conv = conv_ref[...]
@@ -43,31 +140,56 @@
     sig = 1.0 / (1.0 + jnp.exp(-u))
     act = u * sig
     act_hi, act_lo = split(act)
-    cumc = cumc_ref[0]
+    cumr = cumr_ref[...]
+    delr = delr_ref[...]
+    cumc = cumr.T
+    delc8 = delr.T[:8]
     weight = wt_ref[...]
+    wrow = wrow_ref[...]
     score = score_ref[0]
+    score_t = scoret_ref[0] * wrow
     cot = cot_ref[...]
+    pair = 2 * head_size
+    first = lax.broadcasted_iota(jnp.int32, (1, pair), 1) < head_size
     parts, dvals = [], []
-    dscore = jnp.zeros((rows, 8), f32)
-    for h in range(heads):
-        lanes = slice(h * head_size, (h + 1) * head_size)
-        gap = cumc[:, h : h + 1] - cumr_ref[0, h : h + 1, :]
-        decay = jnp.exp(jnp.minimum(gap, 0.0)) * delr_ref[0, h : h + 1, :]
-        mix = decay * score
-        mix_hi, mix_lo = split(mix)
-        hi, lo = act_hi[:, lanes], act_lo[:, lanes]
-        wide = dot(mix_hi, jnp.concatenate([hi, lo], axis=1), ((1,), (0,)))
-        part = wide[:, :head_size] + wide[:, head_size:] + dot(mix_lo, hi, ((1,), (0,)))
-        parts.append(part)
-        mw_hi, mw_lo = split(mix[:, :8] * weight)
-        cot_h = cot[:, lanes]
-        both = dot(jnp.concatenate([mw_hi, mw_lo], axis=1), cot_h, ((0,), (0,)))
-        dvals.append(both[:8] + both[8:])
-        q = dot(cot_h, hi[:8], ((1,), (1,))) + dot(cot_h, lo[:8], ((1,), (1,)))
-        dscore = dscore + decay[:, :8] * q
+    dscore = jnp.zeros((8, rows), f32)
+    for p in range(heads // 2):
+        lanes = slice(p * pair, (p + 1) * pair)
+        lhs, grads, decays = [], [], []
+        for h in (2 * p, 2 * p + 1):
+            gap = cumc[:, h : h + 1] - cumr[h : h + 1, :]
+            mix = jnp.exp(jnp.minimum(gap, 0.0)) * delr[h : h + 1, :] * score
+            lhs.extend(split(mix))
+            gap8 = cumr[h : h + 1, :] - cumc[:8, h : h + 1]
+            decay8 = jnp.exp(jnp.minimum(gap8, 0.0)) * delc8[:, h : h + 1]
+            decays.append(decay8)
+            mix8 = decay8 * score_t
+            hi8 = mix8.astype(bf16).astype(f32)
+            grads.extend([hi8, mix8 - hi8])
+        wide = dot(
+            jnp.concatenate(lhs, axis=0),
+            jnp.concatenate([act_hi[:, lanes], act_lo[:, lanes]], axis=1),
+            ((1,), (0,)),
+        )
+        even = wide[:rows, :pair] + wide[:rows, pair:] + wide[rows : 2 * rows, :pair]
+        odd = wide[2 * rows : 3 * rows, :pair] + wide[2 * rows : 3 * rows, pair:] + wide[3 * rows :, :pair]
+        parts.append(jnp.where(first, even, odd))
+        cot_p = cot[:, lanes]
+        both = dot(jnp.concatenate(grads, axis=0).astype(bf16), cot_p, ((1,), (0,)))
+        dvals.append(jnp.where(first, both[:8] + both[8:16], both[16:24] + both[24:]))
+        a8 = act[:8, lanes]
+        h8 = a8.astype(bf16).astype(f32)
+        l8 = a8 - h8
+        zero = jnp.zeros_like(a8)
+        picks = jnp.concatenate(
+            [jnp.where(first, h8, zero), jnp.where(first, l8, zero),
+             jnp.where(first, zero, h8), jnp.where(first, zero, l8)], axis=0,
+        ).astype(bf16)
+        q = dot(picks, cot_p, ((1,), (1,)))
+        dscore = dscore + decays[0] * (q[:8] + q[8:16]) + decays[1] * (q[16:24] + q[24:])
     skip = skip_ref[...]
     y_ref[...] = jnp.concatenate(parts, axis=1) + skip * act
-    dscore = dscore * weight
+    dscore = dscore * wrow
 
     @pl.when(lax.rem(j, blocks_per_group) == 0)
     def _():
@@ -90,7 +212,7 @@
 
 
 def carried_kernel(
-    blocks_per_group, head_size, own, y_ref, cot_ref, cumc_ref, wt_ref, cc_ref, state_ref, out_ref, dc_ref
+    blocks_per_group, head_size, own, y_ref, cot_ref, cumr_ref, wt_ref, cc_ref, state_ref, out_ref, dc_ref
 ):
     j = pl.program_id(0)
     state_size = state_ref.shape[2]
@@ -99,7 +221,7 @@
     carried = dot(cc[:, :state_size], state, ((1,), (1,))) + dot(
         cc[:, state_size:], state, ((1,), (1,))
     )
-    gains = jnp.exp(cumc_ref[0])
+    gains = jnp.exp(cumr_ref[...]).T
     wide = widen(gains, head_size)
     out_ref[...] = (y_ref[...] + wide * carried).astype(bf16)
     z = cot_ref[...][:8].astype(f32) * (wide[:8] * wt_ref[...][:8])
@@ -141,7 +263,9 @@
     prompt_ids = jnp.arange(prompt_count, dtype=jnp.int32)
 
     small = jnp.concatenate([prompt_tails.reshape(-1).astype(f32), rewards.astype(f32)])
-    small = spread(jnp.pad(small, (0, -small.shape[0] % 128)), device_count)
+    small = jnp.pad(small, (0, -small.shape[0] % 1024)).reshape(1, -1, 128)
+    small = jnp.broadcast_to(small, (device_count,) + small.shape[1:])
+    small = exchange(small, device_count, 1).reshape(device_count, -1)
     states = spread(prompt_states.reshape(width, state_size), device_count)
 
     matches = owners[:, :, None] == holder_ids[None, None, :]
@@ -162,35 +286,30 @@
     tails = jnp.dot(pick, small[:, :tail_len], precision=highest)
     tails = tails.reshape(resp_count, lags, tail_width).transpose(1, 0, 2).reshape(lags, -1)
 
-    bc_ext = jnp.concatenate([tails[:, inner:], bc_input.astype(f32)], axis=0)
-    bc_conv = conv_weight[:, inner:]
-    bc_u = bc_conv[0][None] * bc_ext[0:rows]
-    for k in range(1, lags + 1):
-        bc_u = bc_u + bc_conv[k][None] * bc_ext[k : k + rows]
-    bc_act = jax.nn.silu(bc_u)
+    tail8 = jnp.pad(tails, ((8 - lags, 0), (0, 0)))
+    causal = jnp.arange(rows)[:, None] >= jnp.arange(rows)[None, :]
+    cumr, delr, scores, scores_t, cc, bc_act, bc_u = pl.pallas_call(
+        lambda *refs: prepare_kernel(groups, state_size, lags, *refs),
+        out_shape=[
+            jax.ShapeDtypeStruct((heads, rows), f32),
+            jax.ShapeDtypeStruct((heads, rows), f32),
+            jax.ShapeDtypeStruct((groups, rows, rows), f32),
+            jax.ShapeDtypeStruct((groups, 8, rows), f32),
+            jax.ShapeDtypeStruct((groups, rows, 2 * state_size), bf16),
+            jax.ShapeDtypeStruct((rows, 2 * group_width), f32),
+            jax.ShapeDtypeStruct((8, 2 * group_width), f32),
+        ],
+        scratch_shapes=[pltpu.VMEM((rows + 8, 2 * group_width), f32)],
+        compiler_params=pltpu.CompilerParams(vmem_limit_bytes=24 << 20),
+        name="prepare",
+    )(dt_input, dt_bias[None, :], decay_log[None, :], bc_input, tail8[:, inner:], conv_weight[:, inner:])
     b_proj = bc_act[:, :group_width].reshape(rows, groups, state_size)
     c_proj = bc_act[:, group_width:].reshape(rows, groups, state_size)
-    causal = jnp.arange(rows)[:, None] >= jnp.arange(rows)[None, :]
-    scores = jnp.einsum("tgn,sgn->gts", c_proj, b_proj, precision=highest)
-    scores = jnp.where(causal[None], scores, 0.0)
-    c_group = c_proj.transpose(1, 0, 2)
-    c_hi, c_lo = split(c_group)
-    cc = jnp.concatenate([c_hi, c_lo], axis=2)
-
-    step_size = jax.nn.softplus(dt_input.astype(f32) + dt_bias[None, :])
-    decrement = -step_size * jnp.exp(decay_log)[None, :]
-    cumulative = jnp.dot(causal.astype(f32), decrement, precision=highest)
-    cumc = cumulative.reshape(rows, resp_count, block_heads).transpose(1, 0, 2)
-    cumr = cumulative.T.reshape(resp_count, block_heads, rows)
-    delr = step_size.T.reshape(resp_count, block_heads, rows)
     skip = jnp.repeat(skip_gain, head_size)[None, :]
-    tail8 = jnp.pad(tails[:, :inner], ((8 - lags, 0), (0, 0)))
-    conv_x = conv_weight[:, :inner]
-    taps = conv_x.shape[0]
+    taps = conv_weight.shape[0]
 
     wide_spec = pl.BlockSpec((rows, width), lambda j, own: (0, j))
-    cumc_spec = pl.BlockSpec((1, rows, block_heads), lambda j, own: (j, 0, 0))
-    row_spec = pl.BlockSpec((1, block_heads, rows), lambda j, own: (j, 0, 0))
+    row_spec = pl.BlockSpec((block_heads, rows), lambda j, own: (j, 0))
     wt_spec = pl.BlockSpec((rows, 1), lambda j, own: (0, 0))
     cc_spec = pl.BlockSpec((1, rows, 2 * state_size), lambda j, own: (j // per_group, 0, 0))
     slot_spec = pl.BlockSpec((1, width, state_size), lambda j, own: (own[j], 0, 0))
@@ -206,19 +325,20 @@
                 wide_spec,
                 eight,
                 pl.BlockSpec((taps, width), lambda j, own: (0, j)),
-                cumc_spec,
                 row_spec,
                 row_spec,
                 wt_spec,
+                pl.BlockSpec((1, rows), lambda j, own: (0, 0)),
                 pl.BlockSpec((1, width), lambda j, own: (0, j)),
                 pl.BlockSpec((1, rows, rows), lambda j, own: (j // per_group, 0, 0)),
+                pl.BlockSpec((1, 8, rows), lambda j, own: (j // per_group, 0, 0)),
                 cc_spec,
             ],
             out_specs=[
                 wide_spec,
                 slot_spec,
                 eight,
-                pl.BlockSpec((1, rows, 8), lambda j, own: (j // per_group, 0, 0)),
+                pl.BlockSpec((1, 8, rows), lambda j, own: (j // per_group, 0, 0)),
             ],
             scratch_shapes=[pltpu.VMEM((rows + 8, width), f32)],
         ),
@@ -226,12 +346,12 @@
             jax.ShapeDtypeStruct((rows, inner), f32),
             jax.ShapeDtypeStruct((device_count, width, state_size), bf16),
             jax.ShapeDtypeStruct((8, inner), f32),
-            jax.ShapeDtypeStruct((groups, rows, 8), f32),
+            jax.ShapeDtypeStruct((groups, 8, rows), f32),
         ],
         compiler_params=pltpu.CompilerParams(vmem_limit_bytes=24 << 20),
         cost_estimate=pl.CostEstimate(flops=3 << 30, bytes_accessed=12 << 20, transcendentals=4 << 20),
         name="within",
-    )(owner_row, x_input, out_cotangent, tail8, conv_x, cumc, cumr, delr, weight, skip, scores, cc)
+    )(owner_row, x_input, out_cotangent, tail8, conv_weight, cumr, delr, weight, weight.T, skip, scores, scores_t, cc)
 
     if prompt_count > 1:
         dstate = jnp.where((held_prompt == my_prompt)[:, None, None], dstate, jnp.zeros_like(dstate))
@@ -242,7 +362,7 @@
         grid_spec=pltpu.PrefetchScalarGridSpec(
             num_scalar_prefetch=1,
             grid=(resp_count,),
-            in_specs=[wide_spec, pl.BlockSpec((16, width), lambda j, own: (0, j)), cumc_spec, wt_spec, cc_spec, slot_spec],
+            in_specs=[wide_spec, pl.BlockSpec((16, width), lambda j, own: (0, j)), row_spec, wt_spec, cc_spec, slot_spec],
             out_specs=[
                 wide_spec,
                 pl.BlockSpec((1, 8, state_size), lambda j, own: (j // per_group, 0, 0)),
@@ -255,11 +375,11 @@
         compiler_params=pltpu.CompilerParams(vmem_limit_bytes=24 << 20),
         cost_estimate=pl.CostEstimate(flops=1 << 30, bytes_accessed=9 << 20, transcendentals=1 << 17),
         name="carried",
-    )(owner_row, y_part, out_cotangent, cumc, weight, cc, states)
-
-    keep = jnp.where(causal[:, :8][None], dscore, 0.0)
-    db = jnp.einsum("gts,gtn->sgn", keep, c_group, precision=highest).reshape(8, group_width)
-    dc = jnp.einsum("gts,sgn->tgn", keep[:, :8], b_proj[:8], precision=highest)
+    )(owner_row, y_part, out_cotangent, cumr, weight, cc, states)
+
+    keep = jnp.where(causal[:, :8].T[None], dscore, 0.0)
+    db = jnp.einsum("gst,tgn->sgn", keep, c_proj, precision=highest).reshape(8, group_width)
+    dc = jnp.einsum("gst,sgn->tgn", keep[:, :, :8], b_proj[:8], precision=highest)
     dc = (dc + dc_state.transpose(1, 0, 2)).reshape(8, group_width)
     sig = jax.nn.sigmoid(bc_u[:8])
     du_bc = jnp.concatenate([db, dc], axis=1) * (sig * (1.0 + bc_u[:8] * (1.0 - sig)))
@@ -270,7 +390,8 @@
     tail_blocks = dtail.reshape(lags, resp_count, tail_width).transpose(1, 0, 2)
     tail_blocks = tail_blocks.reshape(resp_count, tail_len)
     tail_send = jnp.dot(pick.T.astype(bf16), tail_blocks, preferred_element_type=f32).astype(bf16)
-    got_tail = lax.all_to_all(tail_send, "dp", split_axis=0, concat_axis=0, tiled=True)
+    tail_send = jnp.pad(tail_send, ((0, 0), (0, -tail_len % 2048))).reshape(device_count, -1, 128)
+    got_tail = exchange(tail_send, device_count, 2).reshape(device_count, -1)[:, :tail_len]
 
     state_grad = jnp.sum(got.astype(f32), axis=0)
     state_grad = state_grad.reshape(1, block_heads, head_size, state_size)

time: 171 us -> 159 us (0.930)
  the two profiles are of different devices: /device:TPU:13 before, /device:TPU:0 now
where the time goes in v1:
time: 159 us
  Pallas kernels  123 us (77%)
  local copies, waits for them, and re-layouts  14.6 us (9%)
  starting transfers between devices  12 us (8%)
  other arithmetic  4.69 us (3%)
  between operations  3.66 us (2%)
    pallas_call x2, Pallas kernels, exchange(): pl.pallas_call(lambda *refs: exchange_kernel(count, *refs), out_shape=jax...  87.2 us
    pallas_call x1, Pallas kernels, local(): pl.pallas_call(lambda *refs: within_kernel(per_group, head_size, lags, *r...  24.3 us
    unnamed x32, local copies, waits for them, and re-layouts  10.3 us
    pallas_call x1, Pallas kernels, local(): pl.pallas_call(lambda *refs: carried_kernel(per_group, head_size, *refs),...  10.1 us
    all_to_all x1, starting transfers between devices, spread(): lax.all_to_all(jnp.broadcast_to(a[None], (count,) + a.shape), 'dp', split...  7.53 us
    all_to_all x1, starting transfers between devices, local(): got = lax.all_to_all(dstate, 'dp', split_axis=0, concat_axis=0, tiled=True)  4.43 us
  transfers between devices with their start and end apart: 2, of which 0 were waited for; matrix products, arithmetic and copies ran while one was open for 3% of the time, Pallas kernels for 77%

profile of v1, /device:TPU:0, one launch (start us, length us, event | category | flops | bytes accessed | tf_op | source)
XLA Modules:
  0.0 158.5 jit_solution(8035778425497075873)
XLA Ops:
  0.6 2.6 %broadcast_in_dim.68 = bf16[16,512,128]{2,1,0:T(8,128)(2,1)} broadcast(bf16[512,128]{1,0:T(8,128)(2,1)} %bitcast.70), dimensions={1,2} | broadcast | bytes 2228224 | tf_op jit(solution)/shard_map/broadcast_in_dim | solution.py:242
  3.3 7.5 %all-to-all-start = ((bf16[16,512,128]{2,1,0:T(8,128)(2,1)}), bf16[16,512,128]{2,1,0:T(8,128)(2,1)S(1)}, u32[]{:S(2)}, u32[]{:S(2)}) async-start(bf16[16,512,128]{2,1,0:T(8,128)(2,1)} %broadcast_in_dim.68), calls=%async_computation | async-start | bytes 4194304 | tf_op jit(solution)/shard_map/all_to_all | solution.py:241
  11.7 51.5 %exchange.2 = f32[16,16,128]{2,1,0:T(8,128)S(1)} custom-call(f32[16,16,128]{2,1,0:T(8,128)S(1)} %broadcast_in_dim.63.refs_0_), custom_call_target="tpu_custom_call" | custom-call | bytes 12582912 | tf_op jit(solution)/shard_map/exchange/pallas_call | solution.py:70
  63.3 0.7 slice_reduce_fusion
  64.6 0.7 multiply_reduce_fusion
  66.6 0.2 fusion.4
  67.5 1.2 prepare.1
  68.7 1.6 copy-done.2
  70.3 1.6 %copy-done.11 = bf16[128,8192]{1,0:T(8,128)(2,1)S(1)} copy-done((bf16[128,8192]{1,0:T(8,128)(2,1)S(1)}, bf16[128,8192]{1,0:T(8,128)(2,1)}, u32[]{:S(2)}) %copy-start.11) | copy-done | bytes 2097176
  71.9 24.3 %within.1 = (f32[128,8192]{1,0:T(8,128)S(1)}, bf16[16,512,128]{2,1,0:T(8,128)(2,1)S(1)}, f32[8,8192]{1,0:T(8,128)S(1)}, f32[4,8,128]{2,1,0:T(8,128)S(1)}) custom-call(s32[16]{0:T(128)S(1)} %bitcast.59, bf16[128,8192]{1,0:T(8,128)(2,1)S(1)} %copy-done.11, bf16[128,8192]{1,0:T(8,128)(2,1)S(1)} %copy-done.2, f32[8,9216]{1,0:T(8,128)S(1)} %pad.13.refs_3_, ...), custom_call_target="tpu_custom_call" | custom-call | flops 3221225472 | bytes 12582912 | tf_op jit(solution)/shard_map/within/pallas_call | solution.py:318
  96.2 1.9 %copy-done = f32[128,8192]{1,0:T(8,128)} copy-done((f32[128,8192]{1,0:T(8,128)}, f32[128,8192]{1,0:T(8,128)S(1)}, u32[]{:S(2)}) %copy-start) | copy-done | bytes 4194328
  98.1 1.3 copy-done.4
  99.4 4.4 %all-to-all-start.1 = ((bf16[16,512,128]{2,1,0:T(8,128)(2,1)}), bf16[16,512,128]{2,1,0:T(8,128)(2,1)}, u32[]{:S(2)}, u32[]{:S(2)}) async-start(bf16[16,512,128]{2,1,0:T(8,128)(2,1)} %copy-done.4), calls=%async_computation.1 | async-start | bytes 4194304 | tf_op jit(solution)/shard_map/all_to_all | solution.py:358
  103.9 0.3 convolution_bitcast_fusion.1
  104.2 2.2 %copy-done.1 = f32[128,8192]{1,0:T(8,128)S(1)} copy-done((f32[128,8192]{1,0:T(8,128)S(1)}, f32[128,8192]{1,0:T(8,128)}, u32[]{:S(2)}) %copy-start.1) | copy-done | bytes 4194328
  106.4 1.6 %copy-done.3 = bf16[128,8192]{1,0:T(8,128)(2,1)S(1)} copy-done((bf16[128,8192]{1,0:T(8,128)(2,1)S(1)}, bf16[128,8192]{1,0:T(8,128)(2,1)}, u32[]{:S(2)}) %copy-start.3) | copy-done | bytes 2097176
  108.0 10.1 %carried.1 = (bf16[128,8192]{1,0:T(8,128)(2,1)}, f32[4,8,128]{2,1,0:T(8,128)S(1)}) custom-call(s32[16]{0:T(128)S(1)} %bitcast.60, f32[128,8192]{1,0:T(8,128)S(1)} %copy-done.1, bf16[128,8192]{1,0:T(8,128)(2,1)S(1)} %copy-done.3, f32[128,128]{1,0:T(8,128)S(1)} %get-tuple-element.16.refs_5_.refs_3_, f32[128,1]{1,0:T(8,128)S(1)} %select_divide_fusion.refs_7_.refs_4_, ...), custom_call_target="tpu_custom_call" | custom-call | flops 1073741824 | bytes 9437184 | tf_op jit(solution)/shard_map/carried/pallas_call | solution.py:360
  118.1 0.2 fusion.1
  118.4 0.4 convert_reduce_fusion.3
  119.1 0.2 maximum_bitcast_fusion
  119.3 0.1 convolution_convert_fusion
  119.5 35.7 %exchange.3 = bf16[16,16,128]{2,1,0:T(8,128)(2,1)S(1)} custom-call(bf16[16,16,128]{2,1,0:T(8,128)(2,1)S(1)} %bitcast.56), custom_call_target="tpu_custom_call" | custom-call | bytes 12582912 | tf_op jit(solution)/shard_map/exchange/pallas_call | solution.py:70
  155.3 0.7 reshape.119
  155.9 2.6 %convert_reduce_fusion = f32[512,128]{1,0:T(8,128)} fusion(bf16[16,512,128]{2,1,0:T(8,128)(2,1)} %all-to-all-done.1), kind=kLoop, calls=%fused_computation | loop fusion | flops 2031616 | bytes 2359296 | tf_op jit(solution)/shard_map/reduce_sum | solution.py:396
  (49 shorter events, 1.3 us)
Async XLA Ops:
  3.3 8.3 %copy-start.12 = (bf16[1,3,576]{2,1,0:T(4,128)(2,1)S(1)}, bf16[1,3,576]{2,1,0:T(4,128)(2,1)}, u32[]{:S(2)}) copy-start(bf16[1,3,576]{2,1,0:T(4,128)(2,1)} %param.18) | copy-start | bytes 10372
  3.3 63.3 %copy-start.8 = (s32[1,16]{1,0:T(1,128)S(1)}, s32[1,16]{1,0:T(1,128)}, u32[]{:S(2)}) copy-start(s32[1,16]{1,0:T(1,128)} %param.21) | copy-start | bytes 196
  3.3 63.9 %copy-start.6 = (f32[4,9216]{1,0:T(4,128)S(1)}, f32[4,9216]{1,0:T(4,128)}, u32[]{:S(2)}) copy-start(f32[4,9216]{1,0:T(4,128)} %refs_4_.1) | copy-start | bytes 442372
  3.3 63.9 %copy-start.13 = (f32[128]{0:T(128)S(1)}, f32[128]{0:T(128)}, u32[]{:S(2)}) copy-start(f32[128]{0:T(128)} %param.25) | copy-start | bytes 1540
  3.3 96.2 %all-to-all-start = ((bf16[16,512,128]{2,1,0:T(8,128)(2,1)}), bf16[16,512,128]{2,1,0:T(8,128)(2,1)S(1)}, u32[]{:S(2)}, u32[]{:S(2)}) async-start(bf16[16,512,128]{2,1,0:T(8,128)(2,1)} %broadcast_in_dim.68), calls=%async_computation | async-start | bytes 4194304 | tf_op jit(solution)/shard_map/all_to_all | solution.py:241
  10.8 56.7 %copy-start.5 = (bf16[128,1024]{1,0:T(8,128)(2,1)S(1)}, bf16[128,1024]{1,0:T(8,128)(2,1)}, u32[]{:S(2)}) copy-start(bf16[128,1024]{1,0:T(8,128)(2,1)} %refs_3_.1) | copy-start | bytes 786436
  10.8 56.7 %copy-start.7 = (bf16[128,128]{1,0:T(8,128)(2,1)S(1)}, bf16[128,128]{1,0:T(8,128)(2,1)}, u32[]{:S(2)}) copy-start(bf16[128,128]{1,0:T(8,128)(2,1)} %refs_0_.1) | copy-start | bytes 98308
  10.8 56.6 %copy-start.9 = (f32[128]{0:T(128)S(1)}, f32[128]{0:T(128)}, u32[]{:S(2)}) copy-start(f32[128]{0:T(128)} %param.24) | copy-start | bytes 1540
  10.8 56.6 %copy-start.10 = (f32[128]{0:T(128)S(1)}, f32[128]{0:T(128)}, u32[]{:S(2)}) copy-start(f32[128]{0:T(128)} %param.23) | copy-start | bytes 1540
  68.7 1.6 %copy-start.2 = (bf16[128,8192]{1,0:T(8,128)(2,1)S(1)}, bf16[128,8192]{1,0:T(8,128)(2,1)}, u32[]{:S(2)}) copy-start(bf16[128,8192]{1,0:T(8,128)(2,1)} %refs_2_.3) | copy-start | bytes 6291460
  70.3 1.6 %copy-start.11 = (bf16[128,8192]{1,0:T(8,128)(2,1)S(1)}, bf16[128,8192]{1,0:T(8,128)(2,1)}, u32[]{:S(2)}) copy-start(bf16[128,8192]{1,0:T(8,128)(2,1)} %refs_1_.1) | copy-start | bytes 6291460
  96.2 1.9 %copy-start = (f32[128,8192]{1,0:T(8,128)}, f32[128,8192]{1,0:T(8,128)S(1)}, u32[]{:S(2)}) copy-start(f32[128,8192]{1,0:T(8,128)S(1)} %get-tuple-element.21.refs_1_) | copy-start | bytes 12582916
  98.1 1.3 copy-start.4
  99.4 56.5 %all-to-all-start.1 = ((bf16[16,512,128]{2,1,0:T(8,128)(2,1)}), bf16[16,512,128]{2,1,0:T(8,128)(2,1)}, u32[]{:S(2)}, u32[]{:S(2)}) async-start(bf16[16,512,128]{2,1,0:T(8,128)(2,1)} %copy-done.4), calls=%async_computation.1 | async-start | bytes 4194304 | tf_op jit(solution)/shard_map/all_to_all | solution.py:358
  104.2 2.2 %copy-start.1 = (f32[128,8192]{1,0:T(8,128)S(1)}, f32[128,8192]{1,0:T(8,128)}, u32[]{:S(2)}) copy-start(f32[128,8192]{1,0:T(8,128)} %copy-done) | copy-start | bytes 12582916
  106.4 1.6 %copy-start.3 = (bf16[128,8192]{1,0:T(8,128)(2,1)S(1)}, bf16[128,8192]{1,0:T(8,128)(2,1)}, u32[]{:S(2)}) copy-start(bf16[128,8192]{1,0:T(8,128)(2,1)} %refs_2_.3) | copy-start | bytes 6291460

commit v2 on v1

--- a/solution.py
+++ b/solution.py
@@ -237,12 +237,6 @@
         dc_ref[0] += dc
 
 
-def spread(a, count):
-    return lax.all_to_all(
-        jnp.broadcast_to(a[None], (count,) + a.shape), "dp", split_axis=0, concat_axis=0, tiled=True
-    )
-
-
 def local(
     x_input, bc_input, dt_input, out_cotangent, prompt_states, prompt_tails, rewards, lengths,
     owners, conv_weight, decay_log, dt_bias, skip_gain,
@@ -266,12 +260,22 @@
     small = jnp.pad(small, (0, -small.shape[0] % 1024)).reshape(1, -1, 128)
     small = jnp.broadcast_to(small, (device_count,) + small.shape[1:])
     small = exchange(small, device_count, 1).reshape(device_count, -1)
-    states = spread(prompt_states.reshape(width, state_size), device_count)
+    chips = device_count // 2
+    lanes_of = [[2 * i + c for i in range(chips)] for c in range(2)]
+    swap = [(i, i ^ 1) for i in range(device_count)]
+    block, small = lax.optimization_barrier((prompt_states.reshape(1, width, state_size), small))
+    half = lax.all_to_all(
+        jnp.broadcast_to(block, (chips, width, state_size)), "dp", split_axis=0, concat_axis=0,
+        axis_index_groups=lanes_of, tiled=True,
+    )
+    states = jnp.concatenate([half, lax.ppermute(half, "dp", swap)], axis=0)
 
     matches = owners[:, :, None] == holder_ids[None, None, :]
     held_prompt = jnp.sum(jnp.where(matches, prompt_ids[:, None, None], 0), axis=(0, 1))
     my_prompt = jnp.sum(jnp.where(holder_ids == my_index, held_prompt, 0))
     owner_row = jnp.sum(jnp.where((prompt_ids == my_prompt)[:, None], owners, 0), axis=0)
+    core = my_index % 2
+    place = jnp.where(owner_row % 2 == core, 0, chips) + owner_row // 2
     pick = (owner_row[:, None] == holder_ids[None, :]).astype(f32)
 
     member = (held_prompt == my_prompt).astype(f32)
@@ -351,11 +355,16 @@
         compiler_params=pltpu.CompilerParams(vmem_limit_bytes=24 << 20),
         cost_estimate=pl.CostEstimate(flops=3 << 30, bytes_accessed=12 << 20, transcendentals=4 << 20),
         name="within",
-    )(owner_row, x_input, out_cotangent, tail8, conv_weight, cumr, delr, weight, weight.T, skip, scores, scores_t, cc)
+    )(place, x_input, out_cotangent, tail8, conv_weight, cumr, delr, weight, weight.T, skip, scores, scores_t, cc)
 
     if prompt_count > 1:
-        dstate = jnp.where((held_prompt == my_prompt)[:, None, None], dstate, jnp.zeros_like(dstate))
-    got = lax.all_to_all(dstate, "dp", split_axis=0, concat_axis=0, tiled=True)
+        used = jnp.any(place[:, None] == holder_ids[None, :], axis=0)
+        dstate = jnp.where(used[:, None, None], dstate, jnp.zeros_like(dstate))
+    other = lax.ppermute(dstate[chips:], "dp", swap)
+    chip_sums = (dstate[:chips].astype(f32) + other.astype(f32)).astype(bf16)
+    got = lax.all_to_all(
+        chip_sums, "dp", split_axis=0, concat_axis=0, axis_index_groups=lanes_of, tiled=True
+    )
 
     layer_out, dc_state = pl.pallas_call(
         lambda *refs: carried_kernel(per_group, head_size, *refs),
@@ -375,7 +384,7 @@
         compiler_params=pltpu.CompilerParams(vmem_limit_bytes=24 << 20),
         cost_estimate=pl.CostEstimate(flops=1 << 30, bytes_accessed=9 << 20, transcendentals=1 << 17),
         name="carried",
-    )(owner_row, y_part, out_cotangent, cumr, weight, cc, states)
+    )(place, y_part, out_cotangent, cumr, weight, cc, states)
 
     keep = jnp.where(causal[:, :8].T[None], dscore, 0.0)
     db = jnp.einsum("gst,tgn->sgn", keep, c_proj, precision=highest).reshape(8, group_width)

time: 159 us -> 98.8 us (0.62)
  Pallas kernels: 123 us -> 58.7 us
  other arithmetic: 4.69 us -> 8.87 us
  local copies, waits for them, and re-layouts: 14.6 us -> 11.4 us
  waiting for transfers between devices: 0.01 us -> 2.49 us
    pallas_call x2, Pallas kernels: 87.2 us -> 23.3 us  [exchange(): pl.pallas_call(lambda *refs: exchange_kernel(count, *refs), out_shape=jax...]
    unnamed x32 -> x28, local copies, waits for them, and re-layouts: 10.3 us -> 5.89 us
    convert_element_type x0 -> x1, other arithmetic: none -> 2.81 us  [local(): chip_sums = (dstate[:chips].astype(f32) + other.astype(f32)).astype(bf16)]
    ppermute x0 -> x2, waiting for transfers between devices: none -> 2.49 us  [the longest x1 2.48 us: local(): other = lax.ppermute(dstate[chips:], 'dp', swap)]
    concatenate x0 -> x1, other arithmetic: none -> 1.87 us  [local(): states = jnp.concatenate([half, lax.ppermute(half, 'dp', swap)], axis=0)]
  transfers between devices with their start and end apart: 2 -> 4, of which waited for: 0 -> 1; matrix products, arithmetic and copies ran while one was open for 3% -> 10% of each run, Pallas kernels for 77% -> 50%
where the time goes in v2:
time: 98.8 us; the launch traced here: 98.4 us
  Pallas kernels  58.7 us (59%)
  starting transfers between devices  12.4 us (13%)
  local copies, waits for them, and re-layouts  11.4 us (12%)
  other arithmetic  8.87 us (9%)
  between operations  3.63 us (4%)
  waiting for transfers between devices  2.49 us (3%)
    pallas_call x1, Pallas kernels, local(): pl.pallas_call(lambda *refs: within_kernel(per_group, head_size, lags, *r...  24.1 us
    pallas_call x2, Pallas kernels, exchange(): pl.pallas_call(lambda *refs: exchange_kernel(count, *refs), out_shape=jax...  23.3 us
    pallas_call x1, Pallas kernels, local(): pl.pallas_call(lambda *refs: carried_kernel(per_group, head_size, *refs),...  10.1 us
    all_to_all x1, starting transfers between devices, local(): lax.all_to_all(chip_sums, 'dp', split_axis=0, concat_axis=0, axis_index_g...  6 us
    all_to_all x1, starting transfers between devices, local(): lax.all_to_all(jnp.broadcast_to(block, (chips, width, state_size)), 'dp',...  5.9 us
    unnamed x28, local copies, waits for them, and re-layouts  5.89 us
    convert_element_type x1, other arithmetic, local(): chip_sums = (dstate[:chips].astype(f32) + other.astype(f32)).astype(bf16)  2.81 us
    ppermute x1, waiting for transfers between devices, local(): other = lax.ppermute(dstate[chips:], 'dp', swap)  2.48 us
  transfers between devices with their start and end apart: 4, of which 1 were waited for; matrix products, arithmetic and copies ran while one was open for 10% of the time, Pallas kernels for 50%

profile of v2, /device:TPU:0, one launch (start us, length us, event | category | flops | bytes accessed | tf_op | source)
XLA Modules:
  0.0 98.4 jit_solution(6160826833316841847)
XLA Ops:
  1.3 0.8 reshape.123
  2.2 9.6 %exchange.2 = f32[16,16,128]{2,1,0:T(8,128)S(1)} custom-call(f32[16,16,128]{2,1,0:T(8,128)S(1)} %broadcast_in_dim.70.refs_0_), custom_call_target="tpu_custom_call" | custom-call | bytes 12582912 | tf_op jit(solution)/shard_map/exchange/pallas_call | solution.py:70
  11.9 2.1 %broadcast_in_dim.75 = bf16[8,512,128]{2,1,0:T(8,128)(2,1)} broadcast(bf16[512,128]{1,0:T(8,128)(2,1)} %bitcast.66), dimensions={1,2} | broadcast | bytes 1179648 | tf_op jit(solution)/shard_map/broadcast_in_dim | solution.py:268
  14.0 5.9 %all-to-all-start = ((bf16[8,512,128]{2,1,0:T(8,128)(2,1)}), bf16[8,512,128]{2,1,0:T(8,128)(2,1)}, u32[]{:S(2)}, u32[]{:S(2)}) async-start(bf16[8,512,128]{2,1,0:T(8,128)(2,1)} %broadcast_in_dim.75), calls=%async_computation | async-start | bytes 2097152 | tf_op jit(solution)/shard_map/all_to_all | solution.py:267
  19.9 0.7 slice_reduce_fusion
  21.4 0.7 multiply_reduce_fusion
  24.1 1.2 %prepare.1 = (f32[128,128]{1,0:T(8,128)S(1)}, f32[128,128]{1,0:T(8,128)S(1)}, f32[4,128,128]{2,1,0:T(8,128)S(1)}, f32[4,8,128]{2,1,0:T(8,128)S(1)}, bf16[4,128,2...) custom-call(bf16[128,128]{1,0:T(8,128)(2,1)S(1)} %copy-done.6, f32[1,128]{1,0:T(1,128)S(1)} %bitcast.58, ...), custom_call_target="tpu_custom_call" | custom-call | tf_op jit(solution)/shard_map/prepare/pallas_call | solution.py:295
  25.4 1.6 %copy-done.9 = bf16[128,8192]{1,0:T(8,128)(2,1)S(1)} copy-done((bf16[128,8192]{1,0:T(8,128)(2,1)S(1)}, bf16[128,8192]{1,0:T(8,128)(2,1)}, u32[]{:S(2)}) %copy-start.9) | copy-done | bytes 2097176
  27.0 24.1 %within.1 = (f32[128,8192]{1,0:T(8,128)S(1)}, bf16[16,512,128]{2,1,0:T(8,128)(2,1)S(1)}, f32[8,8192]{1,0:T(8,128)S(1)}, f32[4,8,128]{2,1,0:T(8,128)S(1)}) custom-call(s32[16]{0:T(128)S(1)} %fusion.14.refs_0_, bf16[128,8192]{1,0:T(8,128)(2,1)S(1)} %copy-done.9, bf16[128,8192]{1,0:T(8,128)(2,1)S(1)} %copy-done.2, f32[8,9216]{1,0:T(8,128)S(1)} %pad.13.refs_3_, ...), custom_call_target="tpu_custom_call" | custom-call | flops 3221225472 | bytes 12582912 | tf_op jit(solution)/shard_map/within/pallas_call | solution.py:322
  51.1 1.9 %copy-done = f32[128,8192]{1,0:T(8,128)} copy-done((f32[128,8192]{1,0:T(8,128)}, f32[128,8192]{1,0:T(8,128)S(1)}, u32[]{:S(2)}) %copy-start) | copy-done | bytes 4194328
  53.0 1.3 %copy-done.3 = bf16[16,512,128]{2,1,0:T(8,128)(2,1)} copy-done((bf16[16,512,128]{2,1,0:T(8,128)(2,1)}, bf16[16,512,128]{2,1,0:T(8,128)(2,1)S(1)}, u32[]{:S(2)}) %copy-start.3) | copy-done | bytes 2097176
  54.3 1.1 %slice.67 = bf16[8,512,128]{2,1,0:T(8,128)(2,1)} slice(bf16[16,512,128]{2,1,0:T(8,128)(2,1)S(1)} %get-tuple-element.27), slice={[8:16], [0:512], [0:128]} | slice | bytes 2097152 | tf_op jit(solution)/shard_map/slice | solution.py:363
  55.4 0.5 collective-permute-start
  55.9 2.5 %collective-permute-done.1 = bf16[8,512,128]{2,1,0:T(8,128)(2,1)} collective-permute-done((bf16[8,512,128]{2,1,0:T(8,128)(2,1)}, bf16[8,512,128]{2,1,0:T(8,128)(2,1)}, u32[]{:S(2)}, u32[]{:S(2)}) %collective-permute-start.1) | collective-permute-done | bytes 1048608 | tf_op jit(solution)/shard_map/ppermute | solution.py:363
  58.4 2.8 %add_convert_fusion = bf16[8,512,128]{2,1,0:T(8,128)(2,1)} fusion(bf16[8,512,128]{2,1,0:T(8,128)(2,1)} %collective-permute-done.1, bf16[16,512,128]{2,1,0:T(8,128)(2,1)} %copy-done.3), kind=kLoop, calls=%fused_computation.3 | loop fusion | flops 2097152 | bytes 3145728 | tf_op jit(solution)/shard_map/convert_element_type | solution.py:364
  61.2 6.0 %all-to-all-start.1 = ((bf16[8,512,128]{2,1,0:T(8,128)(2,1)}), bf16[8,512,128]{2,1,0:T(8,128)(2,1)}, u32[]{:S(2)}, u32[]{:S(2)}) async-start(bf16[8,512,128]{2,1,0:T(8,128)(2,1)} %add_convert_fusion), calls=%async_computation.1 | async-start | bytes 2097152 | tf_op jit(solution)/shard_map/all_to_all | solution.py:365
  67.2 0.3 convolution_bitcast_fusion.1
  67.8 1.9 %pad_maximum_fusion.refs_6_ = bf16[16,512,128]{2,1,0:T(8,128)(2,1)S(1)} fusion(bf16[8,512,128]{2,1,0:T(8,128)(2,1)} %collective-permute-done, bf16[8,512,128]{2,1,0:T(8,128)(2,1)} %all-to-all-done), kind=kLoop, calls=%fused_computation.1 | loop fusion | flops 1048576 | bytes 4194304 | tf_op jit(solution)/shard_map/concatenate | solution.py:271
  69.7 0.9 copy-done.1
  70.6 10.1 %carried.1 = (bf16[128,8192]{1,0:T(8,128)(2,1)}, f32[4,8,128]{2,1,0:T(8,128)S(1)}) custom-call(s32[16]{0:T(128)S(1)} %fusion.14.refs_0_, f32[128,8192]{1,0:T(8,128)S(1)} %copy-done.1, bf16[128,8192]{1,0:T(8,128)(2,1)S(1)} %copy-done.2, f32[128,128]{1,0:T(8,128)S(1)} %get-tuple-element.19.refs_5_.refs_3_, f32[128,1]{1,0:T(8,128)S(1)} %select_divide_fusion.refs_7_.refs_4_, ...), custom_call_target="tpu_custom_call" | custom-call | flops 1073741824 | bytes 9437184 | tf_op jit(solution)/shard_map/carried/pallas_call | solution.py:369
  80.7 0.4 convert_reduce_fusion.3
  81.9 13.7 %exchange.3 = bf16[16,16,128]{2,1,0:T(8,128)(2,1)S(1)} custom-call(bf16[16,16,128]{2,1,0:T(8,128)(2,1)S(1)} %bitcast.56), custom_call_target="tpu_custom_call" | custom-call | bytes 12582912 | tf_op jit(solution)/shard_map/exchange/pallas_call | solution.py:70
  95.6 0.7 reshape.122
  96.3 2.1 %convert_reduce_fusion = f32[512,128]{1,0:T(8,128)} fusion(bf16[8,512,128]{2,1,0:T(8,128)(2,1)} %all-to-all-done.1), kind=kLoop, calls=%fused_computation.2 | loop fusion | flops 983040 | bytes 1310720 | tf_op jit(solution)/shard_map/reduce_sum | solution.py:405
  (54 shorter events, 2.0 us)
Async XLA Ops:
  0.6 19.9 %copy-start.10 = (s32[1,16]{1,0:T(1,128)S(1)}, s32[1,16]{1,0:T(1,128)}, u32[]{:S(2)}) copy-start(s32[1,16]{1,0:T(1,128)} %param.21) | copy-start | bytes 196
  11.8 11.9 %copy-start.5 = (f32[4,9216]{1,0:T(4,128)S(1)}, f32[4,9216]{1,0:T(4,128)}, u32[]{:S(2)}) copy-start(f32[4,9216]{1,0:T(4,128)} %refs_4_.1) | copy-start | bytes 442372
  11.8 11.9 %copy-start.11 = (f32[128]{0:T(128)S(1)}, f32[128]{0:T(128)}, u32[]{:S(2)}) copy-start(f32[128]{0:T(128)} %param.25) | copy-start | bytes 1540
  13.9 10.1 %copy-start.4 = (bf16[128,1024]{1,0:T(8,128)(2,1)S(1)}, bf16[128,1024]{1,0:T(8,128)(2,1)}, u32[]{:S(2)}) copy-start(bf16[128,1024]{1,0:T(8,128)(2,1)} %refs_3_.1) | copy-start | bytes 786436
  13.9 10.1 %copy-start.6 = (bf16[128,128]{1,0:T(8,128)(2,1)S(1)}, bf16[128,128]{1,0:T(8,128)(2,1)}, u32[]{:S(2)}) copy-start(bf16[128,128]{1,0:T(8,128)(2,1)} %refs_0_.1) | copy-start | bytes 98308
  13.9 10.1 %copy-start.7 = (f32[128]{0:T(128)S(1)}, f32[128]{0:T(128)}, u32[]{:S(2)}) copy-start(f32[128]{0:T(128)} %param.24) | copy-start | bytes 1540
  13.9 10.1 %copy-start.8 = (f32[128]{0:T(128)S(1)}, f32[128]{0:T(128)}, u32[]{:S(2)}) copy-start(f32[128]{0:T(128)} %param.23) | copy-start | bytes 1540
  14.0 11.4 %copy-start.2 = (bf16[128,8192]{1,0:T(8,128)(2,1)S(1)}, bf16[128,8192]{1,0:T(8,128)(2,1)}, u32[]{:S(2)}) copy-start(bf16[128,8192]{1,0:T(8,128)(2,1)} %refs_2_.3) | copy-start | bytes 6291460
  14.0 41.4 %all-to-all-start = ((bf16[8,512,128]{2,1,0:T(8,128)(2,1)}), bf16[8,512,128]{2,1,0:T(8,128)(2,1)}, u32[]{:S(2)}, u32[]{:S(2)}) async-start(bf16[8,512,128]{2,1,0:T(8,128)(2,1)} %broadcast_in_dim.75), calls=%async_computation | async-start | bytes 2097152 | tf_op jit(solution)/shard_map/all_to_all | solution.py:267
  25.4 1.6 %copy-start.9 = (bf16[128,8192]{1,0:T(8,128)(2,1)S(1)}, bf16[128,8192]{1,0:T(8,128)(2,1)}, u32[]{:S(2)}) copy-start(bf16[128,8192]{1,0:T(8,128)(2,1)} %refs_1_.1) | copy-start | bytes 6291460
  51.1 1.9 %copy-start = (f32[128,8192]{1,0:T(8,128)}, f32[128,8192]{1,0:T(8,128)S(1)}, u32[]{:S(2)}) copy-start(f32[128,8192]{1,0:T(8,128)S(1)} %get-tuple-element.24.refs_1_) | copy-start | bytes 12582916
  53.0 1.3 %copy-start.3 = (bf16[16,512,128]{2,1,0:T(8,128)(2,1)}, bf16[16,512,128]{2,1,0:T(8,128)(2,1)S(1)}, u32[]{:S(2)}) copy-start(bf16[16,512,128]{2,1,0:T(8,128)(2,1)S(1)} %get-tuple-element.27) | copy-start | bytes 6291460
  55.4 3.0 %collective-permute-start.1 = (bf16[8,512,128]{2,1,0:T(8,128)(2,1)}, bf16[8,512,128]{2,1,0:T(8,128)(2,1)}, u32[]{:S(2)}, u32[]{:S(2)}) collective-permute-start(bf16[8,512,128]{2,1,0:T(8,128)(2,1)} %slice.67), channel_id=1, source_target_pairs={{0,1},{1,0},{2,3},{3,2},{4,5},{5,4},{6,7},{7,6},{8,9},{9,8},{10,11... | collective-permute-start | bytes 3145736 | tf_op jit(solution)/shard_map/ppermute | solution.py:363
  55.4 12.4 %collective-permute-start = (bf16[8,512,128]{2,1,0:T(8,128)(2,1)}, bf16[8,512,128]{2,1,0:T(8,128)(2,1)}, u32[]{:S(2)}, u32[]{:S(2)}) collective-permute-start(bf16[8,512,128]{2,1,0:T(8,128)(2,1)} %all-to-all-done), channel_id=1, source_target_pairs={{0,1},{1,0},{2,3},{3,2},{4,5},{5,4},{6,7},{7,6},{8,9},{9,8},{10,11... | collective-permute-start | bytes 3145736 | tf_op jit(solution)/shard_map/ppermute | solution.py:271
  61.2 35.1 %all-to-all-start.1 = ((bf16[8,512,128]{2,1,0:T(8,128)(2,1)}), bf16[8,512,128]{2,1,0:T(8,128)(2,1)}, u32[]{:S(2)}, u32[]{:S(2)}) async-start(bf16[8,512,128]{2,1,0:T(8,128)(2,1)} %add_convert_fusion), calls=%async_computation.1 | async-start | bytes 2097152 | tf_op jit(solution)/shard_map/all_to_all | solution.py:365
  67.8 2.8 %copy-start.1 = (f32[128,8192]{1,0:T(8,128)S(1)}, f32[128,8192]{1,0:T(8,128)}, u32[]{:S(2)}) copy-start(f32[128,8192]{1,0:T(8,128)} %copy-done) | copy-start | bytes 12582916

commit v3 on v2

--- a/solution.py
+++ b/solution.py
@@ -21,8 +21,10 @@
 
 def widen(cols, head_size):
     rows, heads = cols.shape
+    first = lax.broadcasted_iota(jnp.int32, (rows, 2 * head_size), 1) < head_size
     return jnp.concatenate(
-        [jnp.broadcast_to(cols[:, h : h + 1], (rows, head_size)) for h in range(heads)], axis=1
+        [jnp.where(first, cols[:, h : h + 1], cols[:, h + 1 : h + 2]) for h in range(0, heads, 2)],
+        axis=1,
     )
 
 

time: 98.8 us -> 98.8 us (level)
  no operation moved by 1% of the time
where the time goes in v3:
time: 98.8 us; the launch traced here: 98.4 us
  Pallas kernels  58.7 us (59%)
  starting transfers between devices  12.4 us (13%)
  local copies, waits for them, and re-layouts  11.4 us (12%)
  other arithmetic  8.87 us (9%)
  between operations  3.63 us (4%)
  waiting for transfers between devices  2.49 us (3%)
    pallas_call x1, Pallas kernels, local(): pl.pallas_call(lambda *refs: within_kernel(per_group, head_size, lags, *r...  24.1 us
    pallas_call x2, Pallas kernels, exchange(): pl.pallas_call(lambda *refs: exchange_kernel(count, *refs), out_shape=jax...  23.3 us
    pallas_call x1, Pallas kernels, local(): pl.pallas_call(lambda *refs: carried_kernel(per_group, head_size, *refs),...  10.1 us
    all_to_all x1, starting transfers between devices, local(): lax.all_to_all(chip_sums, 'dp', split_axis=0, concat_axis=0, axis_index_g...  6 us
    all_to_all x1, starting transfers between devices, local(): lax.all_to_all(jnp.broadcast_to(block, (chips, width, state_size)), 'dp',...  5.9 us
    unnamed x28, local copies, waits for them, and re-layouts  5.89 us
    convert_element_type x1, other arithmetic, local(): chip_sums = (dstate[:chips].astype(f32) + other.astype(f32)).astype(bf16)  2.81 us
    ppermute x1, waiting for transfers between devices, local(): other = lax.ppermute(dstate[chips:], 'dp', swap)  2.48 us
  transfers between devices with their start and end apart: 4, of which 1 were waited for; matrix products, arithmetic and copies ran while one was open for 10% of the time, Pallas kernels for 50%

profile of v3, /device:TPU:0, one launch (start us, length us, event | category | flops | bytes accessed | tf_op | source)
XLA Modules:
  0.0 98.4 jit_solution(15395718273215281858)
XLA Ops:
  1.3 0.8 reshape.123
  2.2 9.6 %exchange.2 = f32[16,16,128]{2,1,0:T(8,128)S(1)} custom-call(f32[16,16,128]{2,1,0:T(8,128)S(1)} %broadcast_in_dim.70.refs_0_), custom_call_target="tpu_custom_call" | custom-call | bytes 12582912 | tf_op jit(solution)/shard_map/exchange/pallas_call | solution.py:72
  11.9 2.1 %broadcast_in_dim.75 = bf16[8,512,128]{2,1,0:T(8,128)(2,1)} broadcast(bf16[512,128]{1,0:T(8,128)(2,1)} %bitcast.66), dimensions={1,2} | broadcast | bytes 1179648 | tf_op jit(solution)/shard_map/broadcast_in_dim | solution.py:270
  14.0 5.9 %all-to-all-start = ((bf16[8,512,128]{2,1,0:T(8,128)(2,1)}), bf16[8,512,128]{2,1,0:T(8,128)(2,1)}, u32[]{:S(2)}, u32[]{:S(2)}) async-start(bf16[8,512,128]{2,1,0:T(8,128)(2,1)} %broadcast_in_dim.75), calls=%async_computation | async-start | bytes 2097152 | tf_op jit(solution)/shard_map/all_to_all | solution.py:269
  19.9 0.7 slice_reduce_fusion
  21.4 0.7 multiply_reduce_fusion
  24.1 1.2 %prepare.1 = (f32[128,128]{1,0:T(8,128)S(1)}, f32[128,128]{1,0:T(8,128)S(1)}, f32[4,128,128]{2,1,0:T(8,128)S(1)}, f32[4,8,128]{2,1,0:T(8,128)S(1)}, bf16[4,128,2...) custom-call(bf16[128,128]{1,0:T(8,128)(2,1)S(1)} %copy-done.6, f32[1,128]{1,0:T(1,128)S(1)} %bitcast.58, ...), custom_call_target="tpu_custom_call" | custom-call | tf_op jit(solution)/shard_map/prepare/pallas_call | solution.py:297
  25.4 1.6 %copy-done.9 = bf16[128,8192]{1,0:T(8,128)(2,1)S(1)} copy-done((bf16[128,8192]{1,0:T(8,128)(2,1)S(1)}, bf16[128,8192]{1,0:T(8,128)(2,1)}, u32[]{:S(2)}) %copy-start.9) | copy-done | bytes 2097176
  27.0 24.1 %within.1 = (f32[128,8192]{1,0:T(8,128)S(1)}, bf16[16,512,128]{2,1,0:T(8,128)(2,1)S(1)}, f32[8,8192]{1,0:T(8,128)S(1)}, f32[4,8,128]{2,1,0:T(8,128)S(1)}) custom-call(s32[16]{0:T(128)S(1)} %fusion.14.refs_0_, bf16[128,8192]{1,0:T(8,128)(2,1)S(1)} %copy-done.9, bf16[128,8192]{1,0:T(8,128)(2,1)S(1)} %copy-done.2, f32[8,9216]{1,0:T(8,128)S(1)} %pad.13.refs_3_, ...), custom_call_target="tpu_custom_call" | custom-call | flops 3221225472 | bytes 12582912 | tf_op jit(solution)/shard_map/within/pallas_call | solution.py:324
  51.1 1.9 %copy-done = f32[128,8192]{1,0:T(8,128)} copy-done((f32[128,8192]{1,0:T(8,128)}, f32[128,8192]{1,0:T(8,128)S(1)}, u32[]{:S(2)}) %copy-start) | copy-done | bytes 4194328
  53.0 1.3 %copy-done.3 = bf16[16,512,128]{2,1,0:T(8,128)(2,1)} copy-done((bf16[16,512,128]{2,1,0:T(8,128)(2,1)}, bf16[16,512,128]{2,1,0:T(8,128)(2,1)S(1)}, u32[]{:S(2)}) %copy-start.3) | copy-done | bytes 2097176
  54.4 1.1 %slice.67 = bf16[8,512,128]{2,1,0:T(8,128)(2,1)} slice(bf16[16,512,128]{2,1,0:T(8,128)(2,1)S(1)} %get-tuple-element.27), slice={[8:16], [0:512], [0:128]} | slice | bytes 2097152 | tf_op jit(solution)/shard_map/slice | solution.py:365
  55.4 0.5 collective-permute-start
  55.9 2.5 %collective-permute-done.1 = bf16[8,512,128]{2,1,0:T(8,128)(2,1)} collective-permute-done((bf16[8,512,128]{2,1,0:T(8,128)(2,1)}, bf16[8,512,128]{2,1,0:T(8,128)(2,1)}, u32[]{:S(2)}, u32[]{:S(2)}) %collective-permute-start.1) | collective-permute-done | bytes 1048608 | tf_op jit(solution)/shard_map/ppermute | solution.py:365
  58.4 2.8 %add_convert_fusion = bf16[8,512,128]{2,1,0:T(8,128)(2,1)} fusion(bf16[8,512,128]{2,1,0:T(8,128)(2,1)} %collective-permute-done.1, bf16[16,512,128]{2,1,0:T(8,128)(2,1)} %copy-done.3), kind=kLoop, calls=%fused_computation.3 | loop fusion | flops 2097152 | bytes 3145728 | tf_op jit(solution)/shard_map/convert_element_type | solution.py:366
  61.2 6.0 %all-to-all-start.1 = ((bf16[8,512,128]{2,1,0:T(8,128)(2,1)}), bf16[8,512,128]{2,1,0:T(8,128)(2,1)}, u32[]{:S(2)}, u32[]{:S(2)}) async-start(bf16[8,512,128]{2,1,0:T(8,128)(2,1)} %add_convert_fusion), calls=%async_computation.1 | async-start | bytes 2097152 | tf_op jit(solution)/shard_map/all_to_all | solution.py:367
  67.2 0.3 convolution_bitcast_fusion.1
  67.8 1.9 %pad_maximum_fusion.refs_6_ = bf16[16,512,128]{2,1,0:T(8,128)(2,1)S(1)} fusion(bf16[8,512,128]{2,1,0:T(8,128)(2,1)} %collective-permute-done, bf16[8,512,128]{2,1,0:T(8,128)(2,1)} %all-to-all-done), kind=kLoop, calls=%fused_computation.1 | loop fusion | flops 1048576 | bytes 4194304 | tf_op jit(solution)/shard_map/concatenate | solution.py:273
  69.7 0.9 copy-done.1
  70.6 10.1 %carried.1 = (bf16[128,8192]{1,0:T(8,128)(2,1)}, f32[4,8,128]{2,1,0:T(8,128)S(1)}) custom-call(s32[16]{0:T(128)S(1)} %fusion.14.refs_0_, f32[128,8192]{1,0:T(8,128)S(1)} %copy-done.1, bf16[128,8192]{1,0:T(8,128)(2,1)S(1)} %copy-done.2, f32[128,128]{1,0:T(8,128)S(1)} %get-tuple-element.19.refs_5_.refs_3_, f32[128,1]{1,0:T(8,128)S(1)} %select_divide_fusion.refs_7_.refs_4_, ...), custom_call_target="tpu_custom_call" | custom-call | flops 1073741824 | bytes 9437184 | tf_op jit(solution)/shard_map/carried/pallas_call | solution.py:371
  80.7 0.4 convert_reduce_fusion.3
  81.9 13.7 %exchange.3 = bf16[16,16,128]{2,1,0:T(8,128)(2,1)S(1)} custom-call(bf16[16,16,128]{2,1,0:T(8,128)(2,1)S(1)} %bitcast.56), custom_call_target="tpu_custom_call" | custom-call | bytes 12582912 | tf_op jit(solution)/shard_map/exchange/pallas_call | solution.py:72
  95.6 0.7 reshape.122
  96.3 2.1 %convert_reduce_fusion = f32[512,128]{1,0:T(8,128)} fusion(bf16[8,512,128]{2,1,0:T(8,128)(2,1)} %all-to-all-done.1), kind=kLoop, calls=%fused_computation.2 | loop fusion | flops 983040 | bytes 1310720 | tf_op jit(solution)/shard_map/reduce_sum | solution.py:407
  (54 shorter events, 2.0 us)
Async XLA Ops:
  0.6 19.9 %copy-start.10 = (s32[1,16]{1,0:T(1,128)S(1)}, s32[1,16]{1,0:T(1,128)}, u32[]{:S(2)}) copy-start(s32[1,16]{1,0:T(1,128)} %param.21) | copy-start | bytes 196
  11.8 11.9 %copy-start.5 = (f32[4,9216]{1,0:T(4,128)S(1)}, f32[4,9216]{1,0:T(4,128)}, u32[]{:S(2)}) copy-start(f32[4,9216]{1,0:T(4,128)} %refs_4_.1) | copy-start | bytes 442372
  11.8 11.9 %copy-start.11 = (f32[128]{0:T(128)S(1)}, f32[128]{0:T(128)}, u32[]{:S(2)}) copy-start(f32[128]{0:T(128)} %param.25) | copy-start | bytes 1540
  13.9 10.1 %copy-start.4 = (bf16[128,1024]{1,0:T(8,128)(2,1)S(1)}, bf16[128,1024]{1,0:T(8,128)(2,1)}, u32[]{:S(2)}) copy-start(bf16[128,1024]{1,0:T(8,128)(2,1)} %refs_3_.1) | copy-start | bytes 786436
  13.9 10.1 %copy-start.6 = (bf16[128,128]{1,0:T(8,128)(2,1)S(1)}, bf16[128,128]{1,0:T(8,128)(2,1)}, u32[]{:S(2)}) copy-start(bf16[128,128]{1,0:T(8,128)(2,1)} %refs_0_.1) | copy-start | bytes 98308
  13.9 10.1 %copy-start.7 = (f32[128]{0:T(128)S(1)}, f32[128]{0:T(128)}, u32[]{:S(2)}) copy-start(f32[128]{0:T(128)} %param.24) | copy-start | bytes 1540
  13.9 10.1 %copy-start.8 = (f32[128]{0:T(128)S(1)}, f32[128]{0:T(128)}, u32[]{:S(2)}) copy-start(f32[128]{0:T(128)} %param.23) | copy-start | bytes 1540
  14.0 11.4 %copy-start.2 = (bf16[128,8192]{1,0:T(8,128)(2,1)S(1)}, bf16[128,8192]{1,0:T(8,128)(2,1)}, u32[]{:S(2)}) copy-start(bf16[128,8192]{1,0:T(8,128)(2,1)} %refs_2_.3) | copy-start | bytes 6291460
  14.0 41.5 %all-to-all-start = ((bf16[8,512,128]{2,1,0:T(8,128)(2,1)}), bf16[8,512,128]{2,1,0:T(8,128)(2,1)}, u32[]{:S(2)}, u32[]{:S(2)}) async-start(bf16[8,512,128]{2,1,0:T(8,128)(2,1)} %broadcast_in_dim.75), calls=%async_computation | async-start | bytes 2097152 | tf_op jit(solution)/shard_map/all_to_all | solution.py:269
  25.4 1.6 %copy-start.9 = (bf16[128,8192]{1,0:T(8,128)(2,1)S(1)}, bf16[128,8192]{1,0:T(8,128)(2,1)}, u32[]{:S(2)}) copy-start(bf16[128,8192]{1,0:T(8,128)(2,1)} %refs_1_.1) | copy-start | bytes 6291460
  51.1 1.9 %copy-start = (f32[128,8192]{1,0:T(8,128)}, f32[128,8192]{1,0:T(8,128)S(1)}, u32[]{:S(2)}) copy-start(f32[128,8192]{1,0:T(8,128)S(1)} %get-tuple-element.24.refs_1_) | copy-start | bytes 12582916
  53.0 1.3 %copy-start.3 = (bf16[16,512,128]{2,1,0:T(8,128)(2,1)}, bf16[16,512,128]{2,1,0:T(8,128)(2,1)S(1)}, u32[]{:S(2)}) copy-start(bf16[16,512,128]{2,1,0:T(8,128)(2,1)S(1)} %get-tuple-element.27) | copy-start | bytes 6291460
  55.4 3.0 %collective-permute-start.1 = (bf16[8,512,128]{2,1,0:T(8,128)(2,1)}, bf16[8,512,128]{2,1,0:T(8,128)(2,1)}, u32[]{:S(2)}, u32[]{:S(2)}) collective-permute-start(bf16[8,512,128]{2,1,0:T(8,128)(2,1)} %slice.67), channel_id=1, source_target_pairs={{0,1},{1,0},{2,3},{3,2},{4,5},{5,4},{6,7},{7,6},{8,9},{9,8},{10,11... | collective-permute-start | bytes 3145736 | tf_op jit(solution)/shard_map/ppermute | solution.py:365
  55.4 12.4 %collective-permute-start = (bf16[8,512,128]{2,1,0:T(8,128)(2,1)}, bf16[8,512,128]{2,1,0:T(8,128)(2,1)}, u32[]{:S(2)}, u32[]{:S(2)}) collective-permute-start(bf16[8,512,128]{2,1,0:T(8,128)(2,1)} %all-to-all-done), channel_id=1, source_target_pairs={{0,1},{1,0},{2,3},{3,2},{4,5},{5,4},{6,7},{7,6},{8,9},{9,8},{10,11... | collective-permute-start | bytes 3145736 | tf_op jit(solution)/shard_map/ppermute | solution.py:273
  61.2 35.1 %all-to-all-start.1 = ((bf16[8,512,128]{2,1,0:T(8,128)(2,1)}), bf16[8,512,128]{2,1,0:T(8,128)(2,1)}, u32[]{:S(2)}, u32[]{:S(2)}) async-start(bf16[8,512,128]{2,1,0:T(8,128)(2,1)} %add_convert_fusion), calls=%async_computation.1 | async-start | bytes 2097152 | tf_op jit(solution)/shard_map/all_to_all | solution.py:367
  67.8 2.8 %copy-start.1 = (f32[128,8192]{1,0:T(8,128)S(1)}, f32[128,8192]{1,0:T(8,128)}, u32[]{:S(2)}) copy-start(f32[128,8192]{1,0:T(8,128)} %copy-done) | copy-start | bytes 12582916
